TPU v7x, 32 devices: a whole 2x2x4 slice. The times are simulated.
32 devices in a mesh: expert: 4 (over z), dp: 4 (over y, x), pair: 2 (over core).
Axes of the slice: x: 2, y: 2, z: 4, core: 2. Of those that a mesh axis runs over, the one named last changes fastest.
Arguments:
- byte_states: bfloat16 [4096, 2048], P(('expert', 'dp')), may hold values from -6 to 6
- positions: int32 [2048], P(('expert', 'dp')), may hold values from 0 to 4095, as said below
- picks: int32 [2048, 2], P(('expert', 'dp')), may hold values from 0 to 3, all different within a row; in each aligned block of 128 rows (0 to 127, 128 to 255, ...) at most 80 rows name the same one
- cotangent: bfloat16 [2048, 2048], P(('expert', 'dp')), may hold values from -6 to 6
- router_weight: bfloat16 [2048, 4], replicated, may hold values from -0.125 to 0.125
- gate_weight: bfloat16 [4, 2048, 768], P('expert', 'dp', 'pair'), may hold values from -0.125 to 0.125
- up_weight: bfloat16 [4, 2048, 768], P('expert', 'dp', 'pair'), may hold values from -0.125 to 0.125
- down_weight: bfloat16 [4, 2048, 768], P('expert', 'dp', 'pair'), may hold values from -0.21875 to 0.21875
Outputs:
- row_grad: bfloat16 [2048, 2048], P(('expert', 'dp'))
- gate_grad: bfloat16 [4, 2048, 768], P('expert', 'dp', 'pair')
- up_grad: bfloat16 [4, 2048, 768], P('expert', 'dp', 'pair')
Inputs may be any that keep to these rules, and one draw needn't show every extreme that they name: `positions`: Increasing; the j-th block of 128 rows points into the bytes j * 256 to (j + 1) * 256 - 1 and names the first and the last of them. The 2 picks of a row differ; in each aligned block of 128 rows (the rows of one index of expert and dp) no expert is named by more than 80 rows, a bound that some block reaches.
All inputs are finite; a program needn't handle non-finite values.
Results may differ from a plain program's by a relative error of at most 0.011.
Values may be sent and summed in bfloat16 or wider, within the bound.
A program may use at most 64 MiB of HBM per device.

v0:
```python
import jax
import jax.numpy as jnp
from jax import lax
from jax.sharding import PartitionSpec as P


def local(
    byte_states, positions, picks, cotangent, router_weight, gate_weight, up_weight, down_weight
):
    byte_count = byte_states.shape[0]
    row_total = positions.shape[0]
    width = byte_states.shape[1]
    experts = router_weight.shape[1]
    top_count = picks.shape[1]
    capacity = max(2, 5 * row_total * top_count // (4 * experts))
    pick_total = row_total * top_count
    boundary = jnp.take(byte_states, positions % byte_count, axis=0)
    logits = jnp.dot(boundary, router_weight, preferred_element_type=jnp.float32)
    picked = jnp.take_along_axis(logits, picks, axis=1)
    leading = jax.nn.sigmoid(picked[:, 0] - picked[:, 1])
    mixing = jnp.stack([leading, 1.0 - leading], axis=1)
    mix_low = mixing.astype(jnp.bfloat16).reshape(-1)
    flat_picks = picks.reshape(-1)
    expert_ids = jnp.arange(experts, dtype=jnp.int32)
    one_hot = (flat_picks[:, None] == expert_ids[None, :]).astype(jnp.int32)
    slot_rank = jnp.sum(jnp.cumsum(one_hot, axis=0) * one_hot, axis=1) - 1
    target = flat_picks * capacity + slot_rank
    slot_source = jnp.full((experts * capacity,), pick_total, jnp.int32)
    slot_source = slot_source.at[target].set(jnp.arange(pick_total, dtype=jnp.int32))
    is_live = slot_source < pick_total
    clamped = jnp.minimum(slot_source, pick_total - 1)
    source_row = clamped // top_count
    send_rows = jnp.where(is_live[:, None], boundary[source_row], 0).reshape(
        experts, capacity, width
    )
    send_cot = jnp.where(is_live[:, None], cotangent[source_row], 0).reshape(
        experts, capacity, width
    )
    send_mix = jnp.where(is_live, mix_low[clamped], 0).reshape(experts, capacity)
    gate_full, up_full, down_full = (
        lax.all_gather(gate_weight, "dp", axis=1, tiled=True),
        lax.all_gather(up_weight, "dp", axis=1, tiled=True),
        lax.all_gather(down_weight, "dp", axis=1, tiled=True),
    )
    hidden_half = gate_full.shape[2]
    gate_up = jnp.concatenate([gate_full[0], up_full[0]], axis=1)
    down_mat = down_full[0]
    recv_rows, recv_cot, recv_mix = (
        lax.all_to_all(send_rows, "expert", split_axis=0, concat_axis=0, tiled=True),
        lax.all_to_all(send_cot, "expert", split_axis=0, concat_axis=0, tiled=True),
        lax.all_to_all(send_mix, "expert", split_axis=0, concat_axis=0, tiled=True),
    )
    sources = recv_rows.shape[0]
    slot_total = sources * capacity
    expert_rows = recv_rows.reshape(slot_total, width)
    expert_cot = recv_cot.reshape(slot_total, width)
    expert_mix = recv_mix.reshape(slot_total)
    both_pre = jnp.dot(expert_rows, gate_up, preferred_element_type=jnp.float32)
    gate_pre = both_pre[:, :hidden_half]
    up_pre = both_pre[:, hidden_half:]
    sigma = jax.nn.sigmoid(gate_pre)
    activ = gate_pre * sigma
    slope = sigma * (1.0 + gate_pre * (1.0 - sigma))
    hidden = (activ * up_pre).astype(jnp.bfloat16)
    cot_down = jnp.dot(expert_cot, down_mat, preferred_element_type=jnp.float32)
    mix_part = jnp.sum(hidden.astype(jnp.float32) * cot_down, axis=1)
    scaled = (expert_mix.astype(jnp.float32)[:, None] * expert_cot.astype(jnp.float32)).astype(
        jnp.bfloat16
    )
    hidden_grad = jnp.dot(scaled, down_mat, preferred_element_type=jnp.float32)
    gate_pre_grad = (hidden_grad * up_pre * slope).astype(jnp.bfloat16)
    up_pre_grad = (hidden_grad * activ).astype(jnp.bfloat16)
    joined = jnp.concatenate([gate_pre_grad, up_pre_grad], axis=1)
    grad_part = lax.dot_general(
        joined, gate_up, (((1,), (1,)), ((), ())), preferred_element_type=jnp.float32
    )
    weight_sum = lax.psum_scatter(
        lax.dot_general(
            expert_rows, joined, (((0,), (0,)), ((), ())), preferred_element_type=jnp.float32
        ).astype(jnp.bfloat16),
        "dp",
        scatter_dimension=0,
        tiled=True,
    ).astype(jnp.float32)
    gate_grad = weight_sum[:, :hidden_half].astype(jnp.bfloat16)[None]
    up_grad = weight_sum[:, hidden_half:].astype(jnp.bfloat16)[None]
    grad_sum, mix_sum = (
        lax.psum(grad_part.astype(jnp.bfloat16), "pair").astype(jnp.float32),
        lax.psum(mix_part.astype(jnp.bfloat16), "pair").astype(jnp.float32),
    )
    grad_low = grad_sum.astype(jnp.bfloat16).reshape(sources, capacity, width)
    mix_grad_low = mix_sum.astype(jnp.bfloat16).reshape(sources, capacity)
    back_grad, back_mix = (
        lax.all_to_all(grad_low, "expert", split_axis=0, concat_axis=0, tiled=True),
        lax.all_to_all(mix_grad_low, "expert", split_axis=0, concat_axis=0, tiled=True),
    )
    pick_grad = back_grad.reshape(experts * capacity, width)[target]
    row_sum = jnp.sum(pick_grad.reshape(row_total, top_count, width).astype(jnp.float32), axis=1)
    mix_grad = (
        back_mix.reshape(experts * capacity)[target]
        .reshape(row_total, top_count)
        .astype(jnp.float32)
    )
    blended = jnp.sum(mixing * mix_grad, axis=1, keepdims=True)
    logit_grad = mixing * (mix_grad - blended)
    pick_hot = one_hot.reshape(row_total, top_count, experts).astype(jnp.float32)
    coeffs = jnp.sum(logit_grad[:, :, None] * pick_hot, axis=1)
    router_term = jnp.dot(
        coeffs, router_weight.astype(jnp.float32).T, precision=lax.Precision.HIGHEST
    )
    row_grad = (row_sum + router_term).astype(jnp.bfloat16)
    return (row_grad, gate_grad, up_grad)


def solution(mesh):
    in_specs = (
        P(("expert", "dp"), None),
        P(("expert", "dp")),
        P(("expert", "dp"), None),
        P(("expert", "dp"), None),
        P(),
        P("expert", "dp", "pair"),
        P("expert", "dp", "pair"),
        P("expert", "dp", "pair"),
    )
    out_specs = (P(("expert", "dp"), None), P("expert", "dp", "pair"), P("expert", "dp", "pair"))
    return jax.shard_map(local, mesh=mesh, in_specs=in_specs, out_specs=out_specs, check_vma=False)
```

profile of v0, /device:TPU:9, one launch (start us, length us, event | category | flops | bytes accessed | tf_op | source)
XLA Modules:
  0.0 192.2 jit_solution(4045084865036026282)
XLA Ops:
  14.4 2.4 %gather_fusion.6 = f32[256]{0:T(256)S(1)} fusion(f32[128,4]{0,1:T(4,128)S(1)} %fusion.24, s32[256]{0:T(256)S(1)} %reshape.236), kind=kCustom, calls=%fused_computation.6 | custom fusion | bytes 4096 | tf_op jit(solution)/shard_map/jit(take_along_axis)/gather | solution.py:19
  18.9 2.4 %gather_fusion.1 = bf16[320]{0:T(512)(128)(2,1)S(1)} fusion(bf16[256]{0:T(256)(128)(2,1)S(1)} %convert_element_type.93, s32[1024]{0:T(1024)S(1)} %get-tuple-element.18), kind=kCustom, calls=%fused_computation.1 | custom fusion | bytes 2560 | tf_op jit(solution)/shard_map/gather | solution.py:39
  22.0 4.8 %all-to-all-start = ((bf16[4,1,80]{2,1,0:T(2,128)(2,1)}), bf16[4,1,80]{2,1,0:T(2,128)(2,1)S(1)}, u32[]{:S(2)}, u32[]{:S(2)}) async-start(bf16[4,1,80]{2,1,0:T(2,128)(2,1)} %all_to_all.28), calls=%async_computation | async-start | bytes 4096 | tf_op jit(solution)/shard_map/all_to_all | solution.py:51
  27.6 2.4 %gather_fusion.3 = bf16[320,2048]{1,0:T(8,128)(2,1)S(1)} fusion(bf16[128,2048]{1,0:T(8,128)(2,1)S(1)} %broadcast_select_fusion.2, s32[1024]{0:T(1024)S(1)} %get-tuple-element.17), kind=kCustom, calls=%fused_computation.3 | custom fusion | bytes 2622720 | tf_op jit(solution)/shard_map/gather | solution.py:33
  30.0 3.0 %gather_fusion.2 = bf16[320,2048]{1,0:T(8,128)(2,1)} fusion(bf16[128,2048]{1,0:T(8,128)(2,1)S(1)} %copy-done.1, s32[1024]{0:T(1024)S(1)} %get-tuple-element.17), kind=kCustom, calls=%fused_computation.2 | custom fusion | bytes 2622720 | tf_op jit(solution)/shard_map/gather | solution.py:36
  33.0 3.1 %broadcast_select_fusion = (bf16[4,80,2048]{2,1,0:T(8,128)(2,1)}, bf16[4,80,2048]{2,1,0:T(8,128)(2,1)}) fusion(bf16[4,80,2048]{2,1,0:T(8,128)(2,1)S(1)} %bitcast.57, pred[4,80]{1,0:T(4,128)(4,1)S(1)} %broadcast_in_dim.66, bf16[4,80,2048]{2,1,0:T(8,128)(2,1)} %bitcast.58), kind=kLoop, calls=%fused_computation.19 | loop fusion | flops 1310720 | bytes 5243200 | tf_op jit(solution)/shard_map/jit(_where)/select_n | solution.py:33
  36.1 4.5 %all-to-all-start.1 = ((bf16[4,80,2048]{2,1,0:T(8,128)(2,1)}), bf16[4,80,2048]{2,1,0:T(8,128)(2,1)S(1)}, u32[]{:S(2)}, u32[]{:S(2)}) async-start(bf16[4,80,2048]{2,1,0:T(8,128)(2,1)} %get-tuple-element.16), calls=%async_computation.1 | async-start | bytes 2621440 | tf_op jit(solution)/shard_map/all_to_all | solution.py:50
  41.4 26.1 %all-to-all-done.1 = bf16[4,80,2048]{2,1,0:T(8,128)(2,1)S(1)} async-done(((bf16[4,80,2048]{2,1,0:T(8,128)(2,1)}), bf16[4,80,2048]{2,1,0:T(8,128)(2,1)S(1)}, u32[]{:S(2)}, u32[]{:S(2)}) %all-to-all-start.1) | async-done | bytes 1310752 | tf_op jit(solution)/shard_map/all_to_all | solution.py:50
  67.5 8.2 %all-to-all-start.2 = ((bf16[4,80,2048]{2,1,0:T(8,128)(2,1)}), bf16[4,80,2048]{2,1,0:T(8,128)(2,1)}, u32[]{:S(2)}, u32[]{:S(2)}) async-start(bf16[4,80,2048]{2,1,0:T(8,128)(2,1)} %get-tuple-element.15), calls=%async_computation.2 | async-start | bytes 2621440 | tf_op jit(solution)/shard_map/all_to_all | solution.py:49
  77.2 25.5 %all-to-all-done.2 = bf16[4,80,2048]{2,1,0:T(8,128)(2,1)} async-done(((bf16[4,80,2048]{2,1,0:T(8,128)(2,1)}), bf16[4,80,2048]{2,1,0:T(8,128)(2,1)}, u32[]{:S(2)}, u32[]{:S(2)}) %all-to-all-start.2) | async-done | bytes 1310752 | tf_op jit(solution)/shard_map/all_to_all | solution.py:49
  102.7 3.5 %fusion.1 = f32[320,768]{1,0:T(8,128)S(1)} fusion(bf16[320,2048]{1,0:T(8,128)(2,1)} %bitcast.10, bf16[2048,384]{1,0:T(8,128)(2,1)} %bitcast.68, bf16[2048,384]{1,0:T(8,128)(2,1)} %bitcast.66), kind=kOutput, calls=%fused_computation.14 | convolution fusion | flops 1012924416 | bytes 5439488 | tf_op jit(solution)/shard_map/dot_general | solution.py:58
  107.7 2.9 %multiply_convert_fusion.3 = (bf16[320,384]{1,0:T(8,128)(2,1)S(1)}, bf16[320,384]{1,0:T(8,128)(2,1)S(1)}) fusion(f32[320,768]{1,0:T(8,128)S(1)} %fusion.1, bf16[320,2048]{1,0:T(8,128)(2,1)} %bitcast.60, bf16[1,2048,384]{2,1,0:T(8,128)(2,1)} %all-gather.4.cloned.1.call-done), kind=kOutput, calls=%fused_computation.27 | convolution fusion | flops 504913920 | bytes 4358144 | tf_op jit(solution)/shard_map/dot_general | solution.py:70
  113.1 4.9 %convolution_convert_fusion = bf16[2048,768]{1,0:T(8,128)(2,1)} fusion(bf16[320,2048]{1,0:T(8,128)(2,1)} %bitcast.10, bf16[320,384]{1,0:T(8,128)(2,1)} %copy-done.7, bf16[320,384]{1,0:T(8,128)(2,1)} %copy-done.6), kind=kOutput, calls=%fused_computation.8 | convolution fusion | flops 1009188864 | bytes 4947968 | tf_op jit(solution)/shard_map/dot_general | solution.py:78
  118.0 2.4 %fusion.9 = bf16[320]{0:T(512)(128)(2,1)S(1)} fusion(bf16[320,2048]{1,0:T(8,128)(2,1)S(1)} %bitcast.56, bf16[1,2048,384]{2,1,0:T(8,128)(2,1)} %all-gather.4.cloned.1.call-done, f32[320,768]{1,0:T(8,128)S(1)} %fusion.1), kind=kOutput, calls=%fused_computation.22 | convolution fusion | flops 504422080 | bytes 3867264 | tf_op jit(solution)/shard_map/dot_general | solution.py:65
  120.4 3.0 %psum.15 = bf16[4,1,80]{2,0,1:T(4,128)(2,1)S(1)} all-reduce(bf16[4,1,80]{2,0,1:T(4,128)(2,1)S(1)} %all_to_all.26), channel_id=1, replica_groups=mesh['expert'=4,'dp'=4,'pair'=2] {'pair'}, use_global_device_ids=true, to_apply=%region_7.8 | all-reduce | flops 320 | bytes 1280 | tf_op jit(solution)/shard_map/psum | solution.py:89
  123.4 8.7 %all_to_all.34 = bf16[4,1,80]{2,1,0:T(2,128)(2,1)S(1)} all-to-all(bf16[4,1,80]{2,1,0:T(2,128)(2,1)S(1)} %copy.83), channel_id=1, replica_groups=mesh['expert'=4,'dp'=4,'pair'=2] {'expert'}, dimensions={0} | all-to-all | bytes 1280 | tf_op jit(solution)/shard_map/all_to_all | solution.py:95
  132.1 3.9 %all-reduce.2.cloned.1.call-done = bf16[4,80,2048]{2,1,0:T(8,128)(2,1)} async-done(((bf16[4,80,2048]{2,1,0:T(8,128)(2,1)}), bf16[4,80,2048]{2,1,0:T(8,128)(2,1)}) %all-reduce.2.cloned.1.call-update) | async-done | bytes 1310736 | tf_op jit(solution)/shard_map/psum | solution.py:88
  136.0 4.6 %all-to-all-start.3 = ((bf16[4,80,2048]{2,1,0:T(8,128)(2,1)}), bf16[4,80,2048]{2,1,0:T(8,128)(2,1)S(1)}, u32[]{:S(2)}, u32[]{:S(2)}) async-start(bf16[4,80,2048]{2,1,0:T(8,128)(2,1)} %all-reduce.2.cloned.1.call-done), calls=%async_computation.3 | async-start | bytes 2621440 | tf_op jit(solution)/shard_map/all_to_all | solution.py:94
  142.9 25.6 %all-to-all-done.3 = bf16[4,80,2048]{2,1,0:T(8,128)(2,1)S(1)} async-done(((bf16[4,80,2048]{2,1,0:T(8,128)(2,1)}), bf16[4,80,2048]{2,1,0:T(8,128)(2,1)S(1)}, u32[]{:S(2)}, u32[]{:S(2)}) %all-to-all-start.3) | async-done | bytes 1310752 | tf_op jit(solution)/shard_map/all_to_all | solution.py:94
  168.5 2.3 %gather_fusion.4 = bf16[256,2048]{1,0:T(8,128)(2,1)} fusion(bf16[320,2048]{1,0:T(8,128)(2,1)S(1)} %bitcast.55, s32[1024]{0:T(1024)S(1)} %pad_clamp_fusion), kind=kCustom, calls=%fused_computation.4 | custom fusion | bytes 2098176 | tf_op jit(solution)/shard_map/gather | solution.py:97
  170.9 2.4 %reshape.186 = f32[128,2,2048]{2,1,0:T(2,128)S(1)} reshape(bf16[256,2048]{1,0:T(8,128)(2,1)} %gather_fusion.4) | data formatting | bytes 3145728 | tf_op jit(solution)/shard_map/convert_element_type | solution.py:98
  173.3 3.9 %reduce_sum.46 = f32[128,2048]{1,0:T(8,128)} reduce(f32[128,2,2048]{2,1,0:T(2,128)S(1)} %reshape.186, f32[]{:T(128)} %constant.79.clone.1), dimensions={1}, to_apply=%region_5.6 | reduce | flops 262144 | bytes 3145732 | tf_op jit(solution)/shard_map/reduce_sum | solution.py:98
  177.2 2.7 %fusion = bf16[128,2048]{1,0:T(8,128)(2,1)} fusion(f32[128,2048]{1,0:T(8,128)} %reduce_sum.46, f32[128,4]{0,1:T(4,128)S(1)} %multiply_reduce_fusion, bf16[2048,4]{0,1:T(4,128)(2,1)S(1)} %copy-done.2), kind=kOutput, calls=%fused_computation.13 | convolution fusion | flops 13107200 | bytes 1591296 | tf_op jit(solution)/shard_map/dot_general | solution.py:108
  179.8 3.7 %reduce-scatter.2.cloned.1.call-done = bf16[512,768]{1,0:T(8,128)(2,1)} async-done(((bf16[2048,768]{1,0:T(8,128)(2,1)}), bf16[512,768]{1,0:T(8,128)(2,1)}) %reduce-scatter.2.cloned.1.call-update) | async-done | bytes 786448 | tf_op jit(solution)/shard_map/reduce_scatter | solution.py:77
  (84 shorter events, 21.3 us)
Async XLA Ops:
  7.2 4.4 %copy-start = (bf16[256,2048]{1,0:T(8,128)(2,1)S(1)}, bf16[256,2048]{1,0:T(8,128)(2,1)}, u32[]{:S(2)}) copy-start(bf16[256,2048]{1,0:T(8,128)(2,1)} %param.8) | copy-start | bytes 3145732
  7.2 95.5 %all-gather.6.cloned.1.call-start = ((), (), s32[]{:S(2)}) async-start(), calls=%async_computation.7 | async-start | bytes 1966080 | tf_op jit(solution)/shard_map/all_gather | solution.py:41
  11.6 2.6 %copy-start.2 = (bf16[2048,4]{0,1:T(4,128)(2,1)S(1)}, bf16[2048,4]{0,1:T(4,128)(2,1)}, u32[]{:S(2)}) copy-start(bf16[2048,4]{0,1:T(4,128)(2,1)} %param.12) | copy-start | bytes 49156
  14.4 2.6 %copy-start.3 = (s32[128,2]{0,1:T(2,128)S(1)}, s32[128,2]{0,1:T(2,128)}, u32[]{:S(2)}) copy-start(s32[128,2]{0,1:T(2,128)} %param.10) | copy-start | bytes 3076
  22.0 14.1 %all-to-all-start = ((bf16[4,1,80]{2,1,0:T(2,128)(2,1)}), bf16[4,1,80]{2,1,0:T(2,128)(2,1)S(1)}, u32[]{:S(2)}, u32[]{:S(2)}) async-start(bf16[4,1,80]{2,1,0:T(2,128)(2,1)} %all_to_all.28), calls=%async_computation | async-start | bytes 4096 | tf_op jit(solution)/shard_map/all_to_all | solution.py:51
  26.8 75.9 %all-gather.8.cloned.1.call-start = ((), (), s32[]{:S(2)}) async-start(), calls=%async_computation.8 | async-start | bytes 1966080 | tf_op jit(solution)/shard_map/all_gather | solution.py:42
  27.6 2.4 %copy-start.1 = (bf16[128,2048]{1,0:T(8,128)(2,1)S(1)}, bf16[128,2048]{1,0:T(8,128)(2,1)}, u32[]{:S(2)}) copy-start(bf16[128,2048]{1,0:T(8,128)(2,1)} %param.11) | copy-start | bytes 1572868
  36.1 31.4 %all-to-all-start.1 = ((bf16[4,80,2048]{2,1,0:T(8,128)(2,1)}), bf16[4,80,2048]{2,1,0:T(8,128)(2,1)S(1)}, u32[]{:S(2)}, u32[]{:S(2)}) async-start(bf16[4,80,2048]{2,1,0:T(8,128)(2,1)} %get-tuple-element.16), calls=%async_computation.1 | async-start | bytes 2621440 | tf_op jit(solution)/shard_map/all_to_all | solution.py:50
  40.6 67.1 %all-gather.4.cloned.1.call-start = ((), (), s32[]{:S(2)}) async-start(), calls=%async_computation.6 | async-start | bytes 1966080 | tf_op jit(solution)/shard_map/all_gather | solution.py:43
  67.5 35.2 %all-to-all-start.2 = ((bf16[4,80,2048]{2,1,0:T(8,128)(2,1)}), bf16[4,80,2048]{2,1,0:T(8,128)(2,1)}, u32[]{:S(2)}, u32[]{:S(2)}) async-start(bf16[4,80,2048]{2,1,0:T(8,128)(2,1)} %get-tuple-element.15), calls=%async_computation.2 | async-start | bytes 2621440 | tf_op jit(solution)/shard_map/all_to_all | solution.py:49
  75.8 60.3 %all-reduce.2.cloned.1.call-start = ((), (), s32[]{:S(2)}) async-start(), calls=%async_computation.9 | async-start | bytes 2621440 | tf_op jit(solution)/shard_map/psum | solution.py:88
  107.7 2.9 %copy-start.4 = (bf16[1,2048,384]{2,1,0:T(8,128)(2,1)S(1)}, bf16[1,2048,384]{2,1,0:T(8,128)(2,1)}, u32[]{:S(2)}) copy-start(bf16[1,2048,384]{2,1,0:T(8,128)(2,1)} %all-gather.6.cloned.1.call-done) | copy-start | bytes 4718596
  107.7 2.9 %copy-start.5 = (bf16[1,2048,384]{2,1,0:T(8,128)(2,1)S(1)}, bf16[1,2048,384]{2,1,0:T(8,128)(2,1)}, u32[]{:S(2)}) copy-start(bf16[1,2048,384]{2,1,0:T(8,128)(2,1)} %all-gather.8.cloned.1.call-done) | copy-start | bytes 4718596
  110.6 2.4 %copy-start.6 = (bf16[320,384]{1,0:T(8,128)(2,1)}, bf16[320,384]{1,0:T(8,128)(2,1)S(1)}, u32[]{:S(2)}) copy-start(bf16[320,384]{1,0:T(8,128)(2,1)S(1)} %get-tuple-element.9) | copy-start | bytes 737284
  110.6 2.4 %copy-start.7 = (bf16[320,384]{1,0:T(8,128)(2,1)}, bf16[320,384]{1,0:T(8,128)(2,1)S(1)}, u32[]{:S(2)}) copy-start(bf16[320,384]{1,0:T(8,128)(2,1)S(1)} %get-tuple-element.10) | copy-start | bytes 737284
  113.0 70.6 %reduce-scatter.2.cloned.1.call-start = ((), (), s32[]{:S(2)}) async-start(), calls=%async_computation.10 | async-start | bytes 3932160 | tf_op jit(solution)/shard_map/reduce_scatter | solution.py:77
  136.0 32.5 %all-to-all-start.3 = ((bf16[4,80,2048]{2,1,0:T(8,128)(2,1)}), bf16[4,80,2048]{2,1,0:T(8,128)(2,1)S(1)}, u32[]{:S(2)}, u32[]{:S(2)}) async-start(bf16[4,80,2048]{2,1,0:T(8,128)(2,1)} %all-reduce.2.cloned.1.call-done), calls=%async_computation.3 | async-start | bytes 2621440 | tf_op jit(solution)/shard_map/all_to_all | solution.py:94
Sparse Core Ops, SparseCore 0:
  9.9 32.1 all-gather.5
  43.9 30.9 all-gather.7
  76.7 30.9 all-gather.3
  113.1 22.8 all-reduce.1
  139.1 44.4 reduce-scatter.1
where the time goes:
time: 194 us; the launch traced here: 192 us
  waiting for transfers between devices  88.7 us (46%)
  local copies, waits for them, and re-layouts  24.7 us (13%)
  starting transfers between devices  22.2 us (11%)
  matrix products  18.8 us (10%)
  between operations  14 us (7%)
  other arithmetic  12.1 us (6%)
  blocking collectives  11.7 us (6%)
    all_to_all x1, waiting for transfers between devices, local(): lax.all_to_all(send_cot, 'expert', split_axis=0, concat_axis=0, tiled=True)  26.1 us
    all_to_all x1, waiting for transfers between devices, local(): lax.all_to_all(grad_low, 'expert', split_axis=0, concat_axis=0, tiled=True)  25.6 us
    all_to_all x1, waiting for transfers between devices, local(): lax.all_to_all(send_rows, 'expert', split_axis=0, concat_axis=0, tiled=True)  25.5 us
    all_to_all x1, blocking collectives, local(): lax.all_to_all(mix_grad_low, 'expert', split_axis=0, concat_axis=0, tiled...  8.69 us
    all_to_all x1, starting transfers between devices, local(): lax.all_to_all(send_rows, 'expert', split_axis=0, concat_axis=0, tiled=True)  8.24 us
    dot_general x1, matrix products, local(): lax.dot_general(expert_rows, joined, (((0,), (0,)), ((), ())), preferred_...  4.9 us
    all_to_all x1, starting transfers between devices, local(): lax.all_to_all(send_mix, 'expert', split_axis=0, concat_axis=0, tiled=True)  4.76 us
    all_to_all x1, starting transfers between devices, local(): lax.all_to_all(grad_low, 'expert', split_axis=0, concat_axis=0, tiled=True)  4.58 us
  transfers between devices with their start and end apart: 9, of which 6 were waited for; matrix products, arithmetic and copies ran while one was open for 25% of the time, Pallas kernels for 0%

commit v1 on v0

--- a/solution.py
+++ b/solution.py
@@ -23,7 +23,10 @@
     flat_picks = picks.reshape(-1)
     expert_ids = jnp.arange(experts, dtype=jnp.int32)
     one_hot = (flat_picks[:, None] == expert_ids[None, :]).astype(jnp.int32)
-    slot_rank = jnp.sum(jnp.cumsum(one_hot, axis=0) * one_hot, axis=1) - 1
+    order = jnp.arange(pick_total, dtype=jnp.int32)
+    earlier = (order[None, :] < order[:, None]).astype(jnp.bfloat16)
+    before = jnp.dot(earlier, one_hot.astype(jnp.bfloat16), preferred_element_type=jnp.float32)
+    slot_rank = jnp.sum(before.astype(jnp.int32) * one_hot, axis=1)
     target = flat_picks * capacity + slot_rank
     slot_source = jnp.full((experts * capacity,), pick_total, jnp.int32)
     slot_source = slot_source.at[target].set(jnp.arange(pick_total, dtype=jnp.int32))

time: 194 us -> 193 us (level)
  transfers between devices with their start and end apart: 9 -> 9, of which waited for: 6 -> 6; matrix products, arithmetic and copies ran while one was open for 25% -> 24% of each run, Pallas kernels for 0% -> 0%
where the time goes in v1:
time: 193 us; the launch traced here: 191 us
  waiting for transfers between devices  90 us (47%)
  local copies, waits for them, and re-layouts  24.3 us (13%)
  starting transfers between devices  22.1 us (11%)
  matrix products  19 us (10%)
  between operations  14 us (7%)
  other arithmetic  10.9 us (6%)
  blocking collectives  10.4 us (5%)
    all_to_all x1, waiting for transfers between devices, local(): lax.all_to_all(send_cot, 'expert', split_axis=0, concat_axis=0, tiled=True)  26.3 us
    all_to_all x1, waiting for transfers between devices, local(): lax.all_to_all(grad_low, 'expert', split_axis=0, concat_axis=0, tiled=True)  25.6 us
    all_to_all x1, waiting for transfers between devices, local(): lax.all_to_all(send_rows, 'expert', split_axis=0, concat_axis=0, tiled=True)  25.5 us
    all_to_all x1, starting transfers between devices, local(): lax.all_to_all(send_rows, 'expert', split_axis=0, concat_axis=0, tiled=True)  8.12 us
    all_to_all x1, blocking collectives, local(): lax.all_to_all(mix_grad_low, 'expert', split_axis=0, concat_axis=0, tiled...  7.59 us
    dot_general x1, matrix products, local(): lax.dot_general(expert_rows, joined, (((0,), (0,)), ((), ())), preferred_...  4.88 us
    all_to_all x1, starting transfers between devices, local(): lax.all_to_all(send_mix, 'expert', split_axis=0, concat_axis=0, tiled=True)  4.76 us
    all_to_all x1, starting transfers between devices, local(): lax.all_to_all(grad_low, 'expert', split_axis=0, concat_axis=0, tiled=True)  4.58 us
  transfers between devices with their start and end apart: 9, of which 6 were waited for; matrix products, arithmetic and copies ran while one was open for 24% of the time, Pallas kernels for 0%

profile of v1, /device:TPU:9, one launch (start us, length us, event | category | flops | bytes accessed | tf_op | source)
XLA Modules:
  0.0 190.8 jit_solution(11588501220648236375)
XLA Ops:
  12.7 2.4 %gather_fusion.6 = f32[256]{0:T(256)S(1)} fusion(f32[128,4]{0,1:T(4,128)S(1)} %fusion.25, s32[256]{0:T(256)S(1)} %reshape.214), kind=kCustom, calls=%fused_computation.6 | custom fusion | bytes 4096 | tf_op jit(solution)/shard_map/jit(take_along_axis)/gather | solution.py:19
  17.4 2.4 %gather_fusion.1 = bf16[320]{0:T(512)(128)(2,1)S(1)} fusion(bf16[256]{0:T(256)(128)(2,1)S(1)} %convert_element_type.100, s32[1024]{0:T(1024)S(1)} %get-tuple-element.18), kind=kCustom, calls=%fused_computation.1 | custom fusion | bytes 2560 | tf_op jit(solution)/shard_map/gather | solution.py:42
  20.4 4.8 %all-to-all-start = ((bf16[4,1,80]{2,1,0:T(2,128)(2,1)}), bf16[4,1,80]{2,1,0:T(2,128)(2,1)S(1)}, u32[]{:S(2)}, u32[]{:S(2)}) async-start(bf16[4,1,80]{2,1,0:T(2,128)(2,1)} %all_to_all.28), calls=%async_computation | async-start | bytes 4096 | tf_op jit(solution)/shard_map/all_to_all | solution.py:54
  26.0 2.4 %gather_fusion.3 = bf16[320,2048]{1,0:T(8,128)(2,1)S(1)} fusion(bf16[128,2048]{1,0:T(8,128)(2,1)S(1)} %broadcast_select_fusion.2, s32[1024]{0:T(1024)S(1)} %get-tuple-element.17), kind=kCustom, calls=%fused_computation.3 | custom fusion | bytes 2622720 | tf_op jit(solution)/shard_map/gather | solution.py:36
  28.4 3.0 %gather_fusion.2 = bf16[320,2048]{1,0:T(8,128)(2,1)} fusion(bf16[128,2048]{1,0:T(8,128)(2,1)S(1)} %copy-done.1, s32[1024]{0:T(1024)S(1)} %get-tuple-element.17), kind=kCustom, calls=%fused_computation.2 | custom fusion | bytes 2622720 | tf_op jit(solution)/shard_map/gather | solution.py:39
  31.5 3.2 %broadcast_select_fusion = (bf16[4,80,2048]{2,1,0:T(8,128)(2,1)}, bf16[4,80,2048]{2,1,0:T(8,128)(2,1)}) fusion(bf16[4,80,2048]{2,1,0:T(8,128)(2,1)S(1)} %bitcast.42, pred[4,80]{1,0:T(4,128)(4,1)S(1)} %broadcast_in_dim.68, bf16[4,80,2048]{2,1,0:T(8,128)(2,1)} %bitcast.43), kind=kLoop, calls=%fused_computation.19 | loop fusion | flops 1310720 | bytes 5243200 | tf_op jit(solution)/shard_map/jit(_where)/select_n | solution.py:36
  34.6 4.6 %all-to-all-start.1 = ((bf16[4,80,2048]{2,1,0:T(8,128)(2,1)}), bf16[4,80,2048]{2,1,0:T(8,128)(2,1)S(1)}, u32[]{:S(2)}, u32[]{:S(2)}) async-start(bf16[4,80,2048]{2,1,0:T(8,128)(2,1)} %get-tuple-element.16), calls=%async_computation.1 | async-start | bytes 2621440 | tf_op jit(solution)/shard_map/all_to_all | solution.py:53
  39.9 26.3 %all-to-all-done.1 = bf16[4,80,2048]{2,1,0:T(8,128)(2,1)S(1)} async-done(((bf16[4,80,2048]{2,1,0:T(8,128)(2,1)}), bf16[4,80,2048]{2,1,0:T(8,128)(2,1)S(1)}, u32[]{:S(2)}, u32[]{:S(2)}) %all-to-all-start.1) | async-done | bytes 1310752 | tf_op jit(solution)/shard_map/all_to_all | solution.py:53
  66.2 8.1 %all-to-all-start.2 = ((bf16[4,80,2048]{2,1,0:T(8,128)(2,1)}), bf16[4,80,2048]{2,1,0:T(8,128)(2,1)}, u32[]{:S(2)}, u32[]{:S(2)}) async-start(bf16[4,80,2048]{2,1,0:T(8,128)(2,1)} %get-tuple-element.15), calls=%async_computation.2 | async-start | bytes 2621440 | tf_op jit(solution)/shard_map/all_to_all | solution.py:52
  75.8 25.5 %all-to-all-done.2 = bf16[4,80,2048]{2,1,0:T(8,128)(2,1)} async-done(((bf16[4,80,2048]{2,1,0:T(8,128)(2,1)}), bf16[4,80,2048]{2,1,0:T(8,128)(2,1)}, u32[]{:S(2)}, u32[]{:S(2)}) %all-to-all-start.2) | async-done | bytes 1310752 | tf_op jit(solution)/shard_map/all_to_all | solution.py:52
  101.3 3.5 %fusion.1 = f32[320,768]{1,0:T(8,128)S(1)} fusion(bf16[320,2048]{1,0:T(8,128)(2,1)} %bitcast.8, bf16[2048,384]{1,0:T(8,128)(2,1)} %bitcast.52, bf16[2048,384]{1,0:T(8,128)(2,1)} %bitcast.50), kind=kOutput, calls=%fused_computation.14 | convolution fusion | flops 1012924416 | bytes 5439488 | tf_op jit(solution)/shard_map/dot_general | solution.py:61
  104.7 3.0 %all-gather.4.cloned.1.call-done = bf16[1,2048,384]{2,1,0:T(8,128)(2,1)} async-done(((bf16[1,512,384]{2,1,0:T(8,128)(2,1)}), bf16[1,2048,384]{2,1,0:T(8,128)(2,1)}) %all-gather.4.cloned.1.call-update) | async-done | bytes 1572880 | tf_op jit(solution)/shard_map/all_gather | solution.py:46
  107.7 2.9 %multiply_convert_fusion.3 = (bf16[320,384]{1,0:T(8,128)(2,1)S(1)}, bf16[320,384]{1,0:T(8,128)(2,1)S(1)}) fusion(f32[320,768]{1,0:T(8,128)S(1)} %fusion.1, bf16[320,2048]{1,0:T(8,128)(2,1)} %bitcast.45, bf16[1,2048,384]{2,1,0:T(8,128)(2,1)} %all-gather.4.cloned.1.call-done), kind=kOutput, calls=%fused_computation.30 | convolution fusion | flops 504913920 | bytes 4358144 | tf_op jit(solution)/shard_map/dot_general | solution.py:73
  110.7 2.4 %convolution_convert_fusion.1 = bf16[320,2048]{1,0:T(8,128)(2,1)} fusion(bf16[2048,384]{1,0:T(8,128)(2,1)S(1)} %bitcast.53, bf16[2048,384]{1,0:T(8,128)(2,1)S(1)} %bitcast.51, bf16[320,384]{1,0:T(8,128)(2,1)S(1)} %get-tuple-element.10, bf16[320,384]{1,0:T(8,128)(2,1)S(1)} %get-tuple-element.9), kind=kOutput, calls=%fused_computation.10 | convolution fusion | flops 1014562816 | bytes 4947968 | tf_op jit(solution)/shard_map/dot_general | solution.py:77
  113.1 4.9 %convolution_convert_fusion = bf16[2048,768]{1,0:T(8,128)(2,1)} fusion(bf16[320,2048]{1,0:T(8,128)(2,1)} %bitcast.8, bf16[320,384]{1,0:T(8,128)(2,1)} %copy-done.7, bf16[320,384]{1,0:T(8,128)(2,1)} %copy-done.6), kind=kOutput, calls=%fused_computation.8 | convolution fusion | flops 1009188864 | bytes 4947968 | tf_op jit(solution)/shard_map/dot_general | solution.py:81
  120.5 2.8 %psum.15 = bf16[4,1,80]{2,0,1:T(4,128)(2,1)S(1)} all-reduce(bf16[4,1,80]{2,0,1:T(4,128)(2,1)S(1)} %all_to_all.26), channel_id=1, replica_groups=mesh['expert'=4,'dp'=4,'pair'=2] {'pair'}, use_global_device_ids=true, to_apply=%region_5.6 | all-reduce | flops 320 | bytes 1280 | tf_op jit(solution)/shard_map/psum | solution.py:92
  123.3 7.6 %all_to_all.34 = bf16[4,1,80]{2,1,0:T(2,128)(2,1)S(1)} all-to-all(bf16[4,1,80]{2,1,0:T(2,128)(2,1)S(1)} %copy.66), channel_id=1, replica_groups=mesh['expert'=4,'dp'=4,'pair'=2] {'expert'}, dimensions={0} | all-to-all | bytes 1280 | tf_op jit(solution)/shard_map/all_to_all | solution.py:98
  130.9 3.7 %all-reduce.2.cloned.1.call-done = bf16[4,80,2048]{2,1,0:T(8,128)(2,1)} async-done(((bf16[4,80,2048]{2,1,0:T(8,128)(2,1)}), bf16[4,80,2048]{2,1,0:T(8,128)(2,1)}) %all-reduce.2.cloned.1.call-update) | async-done | bytes 1310736 | tf_op jit(solution)/shard_map/psum | solution.py:91
  134.6 4.6 %all-to-all-start.3 = ((bf16[4,80,2048]{2,1,0:T(8,128)(2,1)}), bf16[4,80,2048]{2,1,0:T(8,128)(2,1)S(1)}, u32[]{:S(2)}, u32[]{:S(2)}) async-start(bf16[4,80,2048]{2,1,0:T(8,128)(2,1)} %all-reduce.2.cloned.1.call-done), calls=%async_computation.3 | async-start | bytes 2621440 | tf_op jit(solution)/shard_map/all_to_all | solution.py:97
  141.5 25.6 %all-to-all-done.3 = bf16[4,80,2048]{2,1,0:T(8,128)(2,1)S(1)} async-done(((bf16[4,80,2048]{2,1,0:T(8,128)(2,1)}), bf16[4,80,2048]{2,1,0:T(8,128)(2,1)S(1)}, u32[]{:S(2)}, u32[]{:S(2)}) %all-to-all-start.3) | async-done | bytes 1310752 | tf_op jit(solution)/shard_map/all_to_all | solution.py:97
  169.5 2.4 %reshape.164 = f32[128,2,2048]{2,1,0:T(2,128)S(1)} reshape(bf16[256,2048]{1,0:T(8,128)(2,1)} %gather_fusion.4) | data formatting | bytes 3145728 | tf_op jit(solution)/shard_map/convert_element_type | solution.py:101
  171.8 3.9 %reduce_sum.49 = f32[128,2048]{1,0:T(8,128)} reduce(f32[128,2,2048]{2,1,0:T(2,128)S(1)} %reshape.164, f32[]{:T(128)} %constant.74.clone.1), dimensions={1}, to_apply=%region_3.4 | reduce | flops 262144 | bytes 3145732 | tf_op jit(solution)/shard_map/reduce_sum | solution.py:101
  175.8 2.7 %fusion = bf16[128,2048]{1,0:T(8,128)(2,1)} fusion(f32[128,2048]{1,0:T(8,128)} %reduce_sum.49, f32[128,4]{0,1:T(4,128)S(1)} %multiply_reduce_fusion, bf16[2048,4]{0,1:T(4,128)(2,1)S(1)} %copy-done.2), kind=kOutput, calls=%fused_computation.13 | convolution fusion | flops 13107200 | bytes 1591296 | tf_op jit(solution)/shard_map/dot_general | solution.py:111
  178.4 3.7 %reduce-scatter.2.cloned.1.call-done = bf16[512,768]{1,0:T(8,128)(2,1)} async-done(((bf16[2048,768]{1,0:T(8,128)(2,1)}), bf16[512,768]{1,0:T(8,128)(2,1)}) %reduce-scatter.2.cloned.1.call-update) | async-done | bytes 786448 | tf_op jit(solution)/shard_map/reduce_scatter | solution.py:80
  (74 shorter events, 20.6 us)
Async XLA Ops:
  7.2 4.2 %copy-start = (bf16[256,2048]{1,0:T(8,128)(2,1)S(1)}, bf16[256,2048]{1,0:T(8,128)(2,1)}, u32[]{:S(2)}) copy-start(bf16[256,2048]{1,0:T(8,128)(2,1)} %param.8) | copy-start | bytes 3145732
  7.2 94.1 %all-gather.6.cloned.1.call-start = ((), (), s32[]{:S(2)}) async-start(), calls=%async_computation.7 | async-start | bytes 1966080 | tf_op jit(solution)/shard_map/all_gather | solution.py:44
  11.4 1.1 copy-start.2
  12.7 2.6 %copy-start.3 = (s32[128,2]{0,1:T(2,128)S(1)}, s32[128,2]{0,1:T(2,128)}, u32[]{:S(2)}) copy-start(s32[128,2]{0,1:T(2,128)} %param.10) | copy-start | bytes 3076
  20.4 14.2 %all-to-all-start = ((bf16[4,1,80]{2,1,0:T(2,128)(2,1)}), bf16[4,1,80]{2,1,0:T(2,128)(2,1)S(1)}, u32[]{:S(2)}, u32[]{:S(2)}) async-start(bf16[4,1,80]{2,1,0:T(2,128)(2,1)} %all_to_all.28), calls=%async_computation | async-start | bytes 4096 | tf_op jit(solution)/shard_map/all_to_all | solution.py:54
  25.2 76.1 %all-gather.8.cloned.1.call-start = ((), (), s32[]{:S(2)}) async-start(), calls=%async_computation.8 | async-start | bytes 1966080 | tf_op jit(solution)/shard_map/all_gather | solution.py:45
  26.0 2.4 %copy-start.1 = (bf16[128,2048]{1,0:T(8,128)(2,1)S(1)}, bf16[128,2048]{1,0:T(8,128)(2,1)}, u32[]{:S(2)}) copy-start(bf16[128,2048]{1,0:T(8,128)(2,1)} %param.11) | copy-start | bytes 1572868
  34.6 31.6 %all-to-all-start.1 = ((bf16[4,80,2048]{2,1,0:T(8,128)(2,1)}), bf16[4,80,2048]{2,1,0:T(8,128)(2,1)S(1)}, u32[]{:S(2)}, u32[]{:S(2)}) async-start(bf16[4,80,2048]{2,1,0:T(8,128)(2,1)} %get-tuple-element.16), calls=%async_computation.1 | async-start | bytes 2621440 | tf_op jit(solution)/shard_map/all_to_all | solution.py:53
  39.2 68.5 %all-gather.4.cloned.1.call-start = ((), (), s32[]{:S(2)}) async-start(), calls=%async_computation.6 | async-start | bytes 1966080 | tf_op jit(solution)/shard_map/all_gather | solution.py:46
  66.2 35.0 %all-to-all-start.2 = ((bf16[4,80,2048]{2,1,0:T(8,128)(2,1)}), bf16[4,80,2048]{2,1,0:T(8,128)(2,1)}, u32[]{:S(2)}, u32[]{:S(2)}) async-start(bf16[4,80,2048]{2,1,0:T(8,128)(2,1)} %get-tuple-element.15), calls=%async_computation.2 | async-start | bytes 2621440 | tf_op jit(solution)/shard_map/all_to_all | solution.py:52
  74.3 60.3 %all-reduce.2.cloned.1.call-start = ((), (), s32[]{:S(2)}) async-start(), calls=%async_computation.9 | async-start | bytes 2621440 | tf_op jit(solution)/shard_map/psum | solution.py:91
  107.7 2.9 %copy-start.4 = (bf16[1,2048,384]{2,1,0:T(8,128)(2,1)S(1)}, bf16[1,2048,384]{2,1,0:T(8,128)(2,1)}, u32[]{:S(2)}) copy-start(bf16[1,2048,384]{2,1,0:T(8,128)(2,1)} %all-gather.6.cloned.1.call-done) | copy-start | bytes 4718596
  107.7 2.9 %copy-start.5 = (bf16[1,2048,384]{2,1,0:T(8,128)(2,1)S(1)}, bf16[1,2048,384]{2,1,0:T(8,128)(2,1)}, u32[]{:S(2)}) copy-start(bf16[1,2048,384]{2,1,0:T(8,128)(2,1)} %all-gather.8.cloned.1.call-done) | copy-start | bytes 4718596
  110.6 2.4 %copy-start.6 = (bf16[320,384]{1,0:T(8,128)(2,1)}, bf16[320,384]{1,0:T(8,128)(2,1)S(1)}, u32[]{:S(2)}) copy-start(bf16[320,384]{1,0:T(8,128)(2,1)S(1)} %get-tuple-element.9) | copy-start | bytes 737284
  110.6 2.4 %copy-start.7 = (bf16[320,384]{1,0:T(8,128)(2,1)}, bf16[320,384]{1,0:T(8,128)(2,1)S(1)}, u32[]{:S(2)}) copy-start(bf16[320,384]{1,0:T(8,128)(2,1)S(1)} %get-tuple-element.10) | copy-start | bytes 737284
  113.1 69.1 %reduce-scatter.2.cloned.1.call-start = ((), (), s32[]{:S(2)}) async-start(), calls=%async_computation.10 | async-start | bytes 3932160 | tf_op jit(solution)/shard_map/reduce_scatter | solution.py:80
  134.6 32.5 %all-to-all-start.3 = ((bf16[4,80,2048]{2,1,0:T(8,128)(2,1)}), bf16[4,80,2048]{2,1,0:T(8,128)(2,1)S(1)}, u32[]{:S(2)}, u32[]{:S(2)}) async-start(bf16[4,80,2048]{2,1,0:T(8,128)(2,1)} %all-reduce.2.cloned.1.call-done), calls=%async_computation.3 | async-start | bytes 2621440 | tf_op jit(solution)/shard_map/all_to_all | solution.py:97
Sparse Core Ops, SparseCore 0:
  9.9 32.1 all-gather.5
  43.9 30.9 all-gather.7
  76.7 30.9 all-gather.3
  113.2 21.3 all-reduce.1
  137.7 44.4 reduce-scatter.1

commit v2 on v1

--- a/solution.py
+++ b/solution.py
@@ -1,7 +1,327 @@
+import functools
+
 import jax
 import jax.numpy as jnp
 from jax import lax
+from jax.experimental import pallas as pl
+from jax.experimental.pallas import tpu as pltpu
 from jax.sharding import PartitionSpec as P
+
+MESH = pl.DeviceIdType.MESH
+LANES = 128
+BF16, F32 = jnp.bfloat16, jnp.float32
+
+
+def dot(a, b, contract=((1,), (0,))):
+    return lax.dot_general(a, b, (contract, ((), ())), preferred_element_type=F32)
+
+
+def kernel(
+    byte_ref, pos_ref, pick_ref, cot_ref, router_ref, gate_ref, up_ref, down_ref,
+    row_out, gate_out, up_out,
+    x_buf, c_buf, w_buf, acc, joined, mix_buf, turn_buf, coef_hi, coef_lo,
+    pick_send, pick_recv, pick_own, line_send, line_recv, wgrad_send, wgrad_recv, fin_send, fin_recv,
+    w_ss, w_rs, z_ss, z_rs, q_ss, q_rs, p_ss, p_rs, l_ss, l_rs, g_ss, g_rs, f_ss, f_rs,
+):
+    z, s, p = lax.axis_index("expert"), lax.axis_index("dp"), lax.axis_index("pair")
+    nz, half, width = x_buf.shape[1], x_buf.shape[2], c_buf.shape[3]
+    depth = gate_ref.shape[1]
+    other = 1 - p
+    x_nb = s + 1 - 2 * lax.rem(s, 2)
+    y_nb = lax.rem(s + 2, 4)
+    diag = 3 - s
+
+    def copy(src, dst, ss, rs, device):
+        return pltpu.make_async_remote_copy(
+            src_ref=src, dst_ref=dst, send_sem=ss, recv_sem=rs, device_id=device, device_id_type=MESH
+        )
+
+    barrier = pltpu.get_barrier_semaphore()
+    peers = [{"dp": x_nb}, {"dp": y_nb}, {"dp": diag}, {"pair": other}]
+    peers += [{"expert": lax.rem(z + j, nz)} for j in range(1, nz)]
+    for peer in peers:
+        pl.semaphore_signal(barrier, inc=1, device_id=peer, device_id_type=MESH)
+
+    spots = lax.broadcasted_iota(jnp.int32, (2 * half, byte_ref.shape[0]), 1)
+    hot = jnp.where(spots == pos_ref[...], 1.0, 0.0).astype(BF16)
+    for c in range(0, width, depth):
+        rows = dot(hot, byte_ref[:, c : c + depth]).astype(BF16)
+        for h in range(2):
+            x_buf[h, z, :, c : c + depth] = rows[h * half : (h + 1) * half]
+    for h in range(2):
+        x_buf[h, z, :, width:] = pick_ref[h * half : (h + 1) * half, :]
+        c_buf[h, z] = cot_ref[h * half : (h + 1) * half, :]
+    pl.semaphore_wait(barrier, len(peers))
+
+    own = [gate_ref.at[0], up_ref.at[0], down_ref.at[0]]
+
+    def w_copy(kind, i):
+        if kind == 0:
+            return copy(own[i], w_buf.at[i, s], w_ss.at[0, i], w_rs.at[0, i], {"dp": x_nb})
+        if kind == 1:
+            return copy(own[i], w_buf.at[i, s], w_ss.at[1, i], w_rs.at[1, i], {"dp": y_nb})
+        part = pl.ds(0 if kind == 2 else depth // 2, depth // 2)
+        frm, to = (x_nb, y_nb) if kind == 2 else (y_nb, x_nb)
+        view = w_buf.at[i, frm, part]
+        return copy(view, view, w_ss.at[kind, i], w_rs.at[kind, i], {"dp": to})
+
+    def w_arrived(kind, i):
+        frm = (x_nb, y_nb, diag, diag)[kind]
+        view = w_buf.at[i, frm]
+        if kind >= 2:
+            view = w_buf.at[i, frm, pl.ds(0 if kind == 2 else depth // 2, depth // 2)]
+        copy(view, view, w_ss.at[kind, i], w_rs.at[kind, i], {"dp": x_nb}).wait_recv()
+
+    for i in range(3):
+        w_copy(0, i).start()
+        w_copy(1, i).start()
+
+    bufs = (c_buf, x_buf)
+
+    def z_copy(up, k, a):
+        origin = lax.rem(z + (nz - k if up else k), nz)
+        view = bufs[a].at[p, origin]
+        d = 0 if up else 1
+        to = lax.rem(z + (1 if up else nz - 1), nz)
+        return copy(view, view, z_ss.at[d, k, a], z_rs.at[d, k, a], {"expert": to})
+
+    def q_copy(up, k, a, mine):
+        origin = lax.rem(z + (nz - k if up else k), nz)
+        view = bufs[a].at[p if mine else other, origin]
+        d = 0 if up else 1
+        return copy(view, view, q_ss.at[d, k - 1, a], q_rs.at[d, k - 1, a], {"pair": other})
+
+    def z_arrived(up, k, a):
+        origin = lax.rem(z + (nz - k if up else k), nz)
+        view = bufs[a].at[p, origin]
+        d = 0 if up else 1
+        to = lax.rem(z + 1, nz)
+        copy(view, view, z_ss.at[d, k - 1, a], z_rs.at[d, k - 1, a], {"expert": to}).wait_recv()
+
+    def comes(up, k):
+        return z >= k if up else z + k < nz
+
+    def goes(up, k):
+        there = z + 1 < nz if up else z >= 1
+        return jnp.logical_and(there, comes(up, k)) if k else there
+
+    for a in range(2):
+        for up in (True, False):
+            pl.when(goes(up, 0))(z_copy(up, 0, a).start)
+
+    def z_step(k):
+        for a in range(2):
+            for up in (True, False):
+
+                def arrived(up=up, a=a):
+                    z_arrived(up, k, a)
+                    q_copy(up, k, a, True).start()
+
+                pl.when(comes(up, k))(arrived)
+                if k + 1 < nz:
+                    pl.when(goes(up, k))(z_copy(up, k, a).start)
+
+    def w_step(i):
+        w_arrived(0, i)
+        w_copy(2, i).start()
+        w_arrived(1, i)
+        w_copy(3, i).start()
+
+    for i in range(3):
+        w_buf[i, s] = own[i][...]
+    w_step(0)
+    z_step(1)
+    w_step(1)
+    z_step(2)
+    w_step(2)
+    z_step(3)
+    for k in range(1, nz):
+        for a in range(2):
+            for up in (True, False):
+                pl.when(comes(up, k))(q_copy(up, k, a, False).wait_recv)
+
+    lane = lax.broadcasted_iota(jnp.int32, (nz * half, LANES), 1).astype(F32)
+    me = z.astype(F32)
+    for h in range(2):
+        logits = dot(x_buf[h, :, :, :width].reshape(nz * half, width), router_ref[...], ((1,), (1,)))
+        meta = x_buf[h, :, :, width:].reshape(nz * half, LANES).astype(F32)
+        first, second = meta[:, 0:1], meta[:, 1:2]
+        hot0 = jnp.where(lane == first, 1.0, 0.0)
+        hot1 = jnp.where(lane == second, 1.0, 0.0)
+        gap = jnp.sum(logits * (hot0 - hot1), axis=1, keepdims=True)
+        leading = jax.nn.sigmoid(gap)
+        rest = 1.0 - leading
+        mixing = jnp.where(first == me, leading, jnp.where(second == me, rest, 0.0))
+        mix_buf[h] = mixing.astype(BF16).astype(F32)
+        sign = jnp.where(first == me, 1.0, jnp.where(second == me, -1.0, 0.0))
+        turn_buf[h] = (leading * rest * sign) * (hot0 - hot1)
+
+    def accumulate(owner, start):
+        cols = pl.ds(pl.multiple_of(owner * depth, depth), depth)
+        for h in range(2):
+            x = x_buf[h, :, :, cols].reshape(nz * half, depth)
+            c = c_buf[h, :, :, cols].reshape(nz * half, depth)
+            for i, rows in enumerate((x, x, c)):
+                term = dot(rows, w_buf[i, owner])
+                acc[i, h] = term if start else acc[i, h] + term
+
+    accumulate(s, True)
+    accumulate(x_nb, False)
+    accumulate(y_nb, False)
+    for i in range(3):
+        w_arrived(2, i)
+        w_arrived(3, i)
+    accumulate(diag, False)
+
+    step = 64
+
+    @pl.loop(0, nz * half // step)
+    def _(n):
+        part = pl.ds(pl.multiple_of(n * step, step), step)
+        for h in range(2):
+            gate, up, cot_down = acc[0, h, part], acc[1, h, part], acc[2, h, part]
+            sigma = jax.nn.sigmoid(gate)
+            activ = gate * sigma
+            slope = sigma * (1.0 + gate * (1.0 - sigma))
+            hidden = (activ * up).astype(BF16).astype(F32)
+            mix_part = jnp.sum(hidden * cot_down, axis=1, keepdims=True)
+            grad = mix_buf[h, part] * cot_down
+            joined[0, h, part] = (grad * up * slope).astype(BF16)
+            joined[1, h, part] = (grad * activ).astype(BF16)
+            coef = mix_part * turn_buf[h, part]
+            high = coef.astype(BF16)
+            coef_hi[h, part] = high
+            coef_lo[h, part] = (coef - high.astype(F32)).astype(BF16)
+
+    def weight_grad(owner, slot):
+        cols = pl.ds(pl.multiple_of(owner * depth, depth), depth)
+        for i in range(2):
+            total = None
+            for h in range(2):
+                x = x_buf[h, :, :, cols].reshape(nz * half, depth)
+                term = dot(x, joined[i, h], ((0,), (0,)))
+                total = term if total is None else total + term
+            wgrad_send[slot, i] = total.astype(BF16)
+
+    def g_copy(slot):
+        to = (x_nb, y_nb, diag)[slot]
+        return copy(wgrad_send.at[slot], wgrad_recv.at[slot], g_ss.at[slot], g_rs.at[slot], {"dp": to})
+
+    for slot in (2, 0, 1):
+        weight_grad((x_nb, y_nb, diag)[slot], slot)
+        g_copy(slot).start()
+
+    def pick_grads(h, c):
+        out = dot(joined[0, h], w_buf[0, c], ((1,), (1,))) + dot(joined[1, h], w_buf[1, c], ((1,), (1,)))
+        router = router_ref[:, c * depth : (c + 1) * depth]
+        return out + dot(coef_hi[h], router) + dot(coef_lo[h], router)
+
+    for c in range(4):
+        pick_send[:, :, c * depth : (c + 1) * depth] = pick_grads(other, c).astype(BF16).reshape(nz, half, depth)
+    p_copy = copy(pick_send, pick_recv, p_ss, p_rs, {"pair": other})
+    p_copy.start()
+    for c in range(4):
+        pick_own[:, :, c * depth : (c + 1) * depth] = pick_grads(p, c).reshape(nz, half, depth)
+    p_copy.wait_recv()
+
+    def l_copy(j):
+        to = lax.rem(z + j, nz)
+        return copy(line_send.at[j - 1], line_recv.at[j - 1], l_ss.at[j - 1], l_rs.at[j - 1], {"expert": to})
+
+    for j in range(1, nz):
+        origin = lax.rem(z + j, nz)
+        line_send[j - 1] = (pick_own[origin] + pick_recv[origin].astype(F32)).astype(BF16)
+        l_copy(j).start()
+    weight_grad(s, 3)
+
+    for j in range(1, nz):
+        l_copy(j).wait_recv()
+    total = pick_own[z] + pick_recv[z].astype(F32)
+    for j in range(1, nz):
+        total = total + line_recv[j - 1].astype(F32)
+    fin_send[...] = total.astype(BF16)
+    f_copy = copy(fin_send, fin_recv, f_ss, f_rs, {"pair": other})
+    f_copy.start()
+    row_out[pl.ds(pl.multiple_of(p * half, half), half), :] = fin_send[...]
+
+    for slot in range(3):
+        g_copy(slot).wait_recv()
+    for i, out in enumerate((gate_out, up_out)):
+        sums = wgrad_send[3, i].astype(F32)
+        for slot in range(3):
+            sums = sums + wgrad_recv[slot, i].astype(F32)
+        out[0] = sums.astype(BF16)
+    f_copy.wait_recv()
+    row_out[pl.ds(pl.multiple_of(other * half, half), half), :] = fin_recv[...]
+
+    for i in range(3):
+        for kind in range(4):
+            w_copy(kind, i).wait_send()
+    for a in range(2):
+        for up in (True, False):
+            for k in range(nz - 1):
+                pl.when(goes(up, k))(z_copy(up, k, a).wait_send)
+            for k in range(1, nz):
+                pl.when(comes(up, k))(q_copy(up, k, a, True).wait_send)
+    for slot in range(3):
+        g_copy(slot).wait_send()
+    p_copy.wait_send()
+    for j in range(1, nz):
+        l_copy(j).wait_send()
+    f_copy.wait_send()
+
+
+def dense(
+    nz, byte_states, positions, picks, cotangent, router_weight, gate_weight, up_weight, down_weight
+):
+    rows, width = cotangent.shape
+    half, depth, units = rows // 2, gate_weight.shape[1], gate_weight.shape[2]
+    spots = (positions % byte_states.shape[0])[:, None]
+    meta = jnp.pad(picks.astype(BF16), ((0, 0), (0, LANES - picks.shape[1])))
+    router = jnp.pad(router_weight.T, ((0, LANES - router_weight.shape[1]), (0, 0)))
+    vmem, dma = pltpu.VMEM, pltpu.SemaphoreType.DMA
+    whole = pl.BlockSpec(memory_space=vmem)
+    scratch = [
+        vmem((2, nz, half, width + LANES), BF16),
+        vmem((2, nz, half, width), BF16),
+        vmem((3, 4, depth, units), BF16),
+        vmem((3, 2, nz * half, units), F32),
+        vmem((2, 2, nz * half, units), BF16),
+        vmem((2, nz * half, 1), F32),
+        vmem((2, nz * half, LANES), F32),
+        vmem((2, nz * half, LANES), BF16),
+        vmem((2, nz * half, LANES), BF16),
+        vmem((nz, half, width), BF16),
+        vmem((nz, half, width), BF16),
+        vmem((nz, half, width), F32),
+        vmem((nz - 1, half, width), BF16),
+        vmem((nz - 1, half, width), BF16),
+        vmem((4, 2, depth, units), BF16),
+        vmem((3, 2, depth, units), BF16),
+        vmem((half, width), BF16),
+        vmem((half, width), BF16),
+        dma((4, 3)), dma((4, 3)),
+        dma((2, nz - 1, 2)), dma((2, nz - 1, 2)),
+        dma((2, nz - 1, 2)), dma((2, nz - 1, 2)),
+        dma, dma,
+        dma((nz - 1,)), dma((nz - 1,)),
+        dma((3,)), dma((3,)),
+        dma, dma,
+    ]
+    return pl.pallas_call(
+        kernel,
+        out_shape=(
+            jax.ShapeDtypeStruct((rows, width), BF16),
+            jax.ShapeDtypeStruct(gate_weight.shape, BF16),
+            jax.ShapeDtypeStruct(up_weight.shape, BF16),
+        ),
+        in_specs=[whole] * 8,
+        out_specs=(whole,) * 3,
+        scratch_shapes=scratch,
+        compiler_params=pltpu.CompilerParams(
+            collective_id=0, has_side_effects=True, vmem_limit_bytes=52 * 2**20
+        ),
+    )(byte_states, spots, meta, cotangent, router, gate_weight, up_weight, down_weight)
 
 
 def local(
@@ -127,4 +447,6 @@
         P("expert", "dp", "pair"),
     )
     out_specs = (P(("expert", "dp"), None), P("expert", "dp", "pair"), P("expert", "dp", "pair"))
-    return jax.shard_map(local, mesh=mesh, in_specs=in_specs, out_specs=out_specs, check_vma=False)
+    few = dict(mesh.shape) == {"expert": 4, "dp": 4, "pair": 2}
+    body = functools.partial(dense, 4) if few else local
+    return jax.shard_map(body, mesh=mesh, in_specs=in_specs, out_specs=out_specs, check_vma=False)

time: 193 us -> 96.4 us (0.50)
  the two profiles are of different devices: /device:TPU:9 before, /device:TPU:0 now
where the time goes in v2:
time: 96.4 us; the launch traced here: 96.1 us
  Pallas kernels  87.8 us (91%)
  local copies, waits for them, and re-layouts  6.2 us (6%)
  other arithmetic  1.4 us (1%)
    pallas_call x1, Pallas kernels, dense(): pl.pallas_call(kernel, out_shape=(jax.ShapeDtypeStruct((rows, width), BF1...  87.8 us
    unnamed x7, local copies, waits for them, and re-layouts  4.37 us

profile of v2, /device:TPU:0, one launch (start us, length us, event | category | flops | bytes accessed | tf_op | source)
XLA Modules:
  0.0 96.1 jit_solution(3533443957392694375)
XLA Ops:
  0.6 0.0 copy-start
  0.6 0.7 fusion
  1.4 0.7 convert_element_type.7
  2.0 0.1 copy.13
  2.2 0.1 copy.14.pos_ref
  2.3 1.6 %pad.9.router_ref = bf16[128,2048]{1,0:T(8,128)(2,1)} pad(bf16[4,2048]{1,0:T(4,128)(2,1)} %bitcast.3, bf16[]{:T(256)} %constant.17.clone.1), padding=0_124x0_0 | pad | bytes 540674 | tf_op jit(solution)/shard_map/jit(_pad)/pad | solution.py:281
  3.9 0.0 copy-done
  3.9 0.0 copy-start.1
  3.9 1.0 %copy-done.1 = bf16[1,512,384]{2,1,0:T(8,128)(2,1)S(1)} copy-done((bf16[1,512,384]{2,1,0:T(8,128)(2,1)S(1)}, bf16[1,512,384]{2,1,0:T(8,128)(2,1)}, u32[]{:S(2)}) %copy-start.1) | copy-done | bytes 393240
  4.9 87.8 %shard_map.103 = (bf16[128,2048]{1,0:T(8,128)(2,1)}, bf16[1,512,384]{2,1,0:T(8,128)(2,1)S(1)}, bf16[1,512,384]{2,1,0:T(8,128)(2,1)S(1)}) custom-call(bf16[256,2048]{1,0:T(8,128)(2,1)} %byte_ref.1, s32[128,1]{1,0:T(8,128)S(1)} %copy.14.pos_ref, bf16[128,128]{1,0:T(8,128)(2,1)S(1)} %pad.8.pick_ref, bf16[128,2048]{1,0:T(8,128)(2,1)} %cot_ref.1, ...), custom_call_target="tpu_custom_call" | custom-call | tf_op jit(solution)/shard_map/pallas_call | solution.py:311
  92.7 1.9 %copy.18 = bf16[128,2048]{1,0:T(8,128)(2,1)} copy(bf16[128,2048]{1,0:T(8,128)(2,1)} %get-tuple-element.6) | data formatting | bytes 1048576
  94.6 0.7 copy.19
  95.4 0.7 copy.20
  (1 shorter events, 0.0 us)
Async XLA Ops:
  0.6 3.2 %copy-start = (bf16[1,512,384]{2,1,0:T(8,128)(2,1)S(1)}, bf16[1,512,384]{2,1,0:T(8,128)(2,1)}, u32[]{:S(2)}) copy-start(bf16[1,512,384]{2,1,0:T(8,128)(2,1)} %gate_ref.1) | copy-start | bytes 1179652
  3.9 1.0 %copy-start.1 = (bf16[1,512,384]{2,1,0:T(8,128)(2,1)S(1)}, bf16[1,512,384]{2,1,0:T(8,128)(2,1)}, u32[]{:S(2)}) copy-start(bf16[1,512,384]{2,1,0:T(8,128)(2,1)} %up_ref.1) | copy-start | bytes 1179652

commit v3 on v2

--- a/solution.py
+++ b/solution.py
@@ -20,7 +20,7 @@
     byte_ref, pos_ref, pick_ref, cot_ref, router_ref, gate_ref, up_ref, down_ref,
     row_out, gate_out, up_out,
     x_buf, c_buf, w_buf, acc, joined, mix_buf, turn_buf, coef_hi, coef_lo,
-    pick_send, pick_recv, pick_own, line_send, line_recv, wgrad_send, wgrad_recv, fin_send, fin_recv,
+    pick_send, pick_recv, pick_own, line_send, line_recv, wgrad_send, wgrad_recv, fin_send, fin_recv, router,
     w_ss, w_rs, z_ss, z_rs, q_ss, q_rs, p_ss, p_rs, l_ss, l_rs, g_ss, g_rs, f_ss, f_rs,
 ):
     z, s, p = lax.axis_index("expert"), lax.axis_index("dp"), lax.axis_index("pair")
@@ -42,14 +42,18 @@
     for peer in peers:
         pl.semaphore_signal(barrier, inc=1, device_id=peer, device_id_type=MESH)
 
-    spots = lax.broadcasted_iota(jnp.int32, (2 * half, byte_ref.shape[0]), 1)
+    count = byte_ref.shape[0]
+    spots = lax.broadcasted_iota(jnp.int32, (count, 2 * half), 0) + (z * 4 + s) * count
     hot = jnp.where(spots == pos_ref[...], 1.0, 0.0).astype(BF16)
     for c in range(0, width, depth):
-        rows = dot(hot, byte_ref[:, c : c + depth]).astype(BF16)
+        rows = dot(hot, byte_ref[:, c : c + depth], ((0,), (0,))).astype(BF16)
         for h in range(2):
             x_buf[h, z, :, c : c + depth] = rows[h * half : (h + 1) * half]
+    place = lax.broadcasted_iota(jnp.int32, (LANES, 2 * half), 0)
+    picked = pick_ref[...].astype(F32)
+    meta = jnp.where(place == 0, picked[0:1, :], jnp.where(place == 1, picked[1:2, :], 0.0)).T
     for h in range(2):
-        x_buf[h, z, :, width:] = pick_ref[h * half : (h + 1) * half, :]
+        x_buf[h, z, :, width:] = meta[h * half : (h + 1) * half].astype(BF16)
         c_buf[h, z] = cot_ref[h * half : (h + 1) * half, :]
     pl.semaphore_wait(barrier, len(peers))
 
@@ -129,11 +133,12 @@
 
     for i in range(3):
         w_buf[i, s] = own[i][...]
-    w_step(0)
+    router[...] = jnp.zeros_like(router)
+    router[: router_ref.shape[0], :] = router_ref[...]
     z_step(1)
-    w_step(1)
     z_step(2)
-    w_step(2)
+    for i in range(3):
+        w_step(i)
     z_step(3)
     for k in range(1, nz):
         for a in range(2):
@@ -143,7 +148,7 @@
     lane = lax.broadcasted_iota(jnp.int32, (nz * half, LANES), 1).astype(F32)
     me = z.astype(F32)
     for h in range(2):
-        logits = dot(x_buf[h, :, :, :width].reshape(nz * half, width), router_ref[...], ((1,), (1,)))
+        logits = dot(x_buf[h, :, :, :width].reshape(nz * half, width), router[...], ((1,), (1,)))
         meta = x_buf[h, :, :, width:].reshape(nz * half, LANES).astype(F32)
         first, second = meta[:, 0:1], meta[:, 1:2]
         hot0 = jnp.where(lane == first, 1.0, 0.0)
@@ -156,13 +161,13 @@
         sign = jnp.where(first == me, 1.0, jnp.where(second == me, -1.0, 0.0))
         turn_buf[h] = (leading * rest * sign) * (hot0 - hot1)
 
-    def accumulate(owner, start):
+    def accumulate(owner, start, which=(0, 1, 2)):
         cols = pl.ds(pl.multiple_of(owner * depth, depth), depth)
         for h in range(2):
             x = x_buf[h, :, :, cols].reshape(nz * half, depth)
             c = c_buf[h, :, :, cols].reshape(nz * half, depth)
-            for i, rows in enumerate((x, x, c)):
-                term = dot(rows, w_buf[i, owner])
+            for i in which:
+                term = dot(c if i == 2 else x, w_buf[i, owner])
                 acc[i, h] = term if start else acc[i, h] + term
 
     accumulate(s, True)
@@ -171,7 +176,7 @@
     for i in range(3):
         w_arrived(2, i)
         w_arrived(3, i)
-    accumulate(diag, False)
+        accumulate(diag, False, (i,))
 
     step = 64
 
@@ -193,7 +198,9 @@
             coef_hi[h, part] = high
             coef_lo[h, part] = (coef - high.astype(F32)).astype(BF16)
 
-    def weight_grad(owner, slot):
+    low, high = pl.ds(0, depth // 2), pl.ds(depth // 2, depth // 2)
+
+    def weight_grad(owner, keep):
         cols = pl.ds(pl.multiple_of(owner * depth, depth), depth)
         for i in range(2):
             total = None
@@ -201,20 +208,43 @@
                 x = x_buf[h, :, :, cols].reshape(nz * half, depth)
                 term = dot(x, joined[i, h], ((0,), (0,)))
                 total = term if total is None else total + term
-            wgrad_send[slot, i] = total.astype(BF16)
-
-    def g_copy(slot):
-        to = (x_nb, y_nb, diag)[slot]
-        return copy(wgrad_send.at[slot], wgrad_recv.at[slot], g_ss.at[slot], g_rs.at[slot], {"dp": to})
-
-    for slot in (2, 0, 1):
-        weight_grad((x_nb, y_nb, diag)[slot], slot)
-        g_copy(slot).start()
+            keep[i] = total.astype(BF16)
+
+    def g_copy(stage):
+        to_x = stage % 2 == 0
+        slot = 2 if stage < 2 else 0 if to_x else 1
+        part = low if stage in (0, 2, 5) else high
+        src = wgrad_send.at[slot, :, part]
+        if stage < 2:
+            dst = wgrad_recv.at[2, :, part]
+        else:
+            dst = wgrad_recv.at[0 if to_x else 1, :, part]
+        return copy(src, dst, g_ss.at[stage], g_rs.at[stage], {"dp": x_nb if to_x else y_nb})
+
+    weight_grad(diag, wgrad_send.at[2])
+    g_copy(0).start()
+    g_copy(1).start()
+    weight_grad(x_nb, wgrad_send.at[0])
+    g_copy(2).start()
+    weight_grad(y_nb, wgrad_send.at[1])
+    g_copy(3).start()
+
+    def pass_on():
+        g_copy(0).wait_recv()
+        for i in range(2):
+            mine = wgrad_send[1, i, low].astype(F32) + wgrad_recv[2, i, low].astype(F32)
+            wgrad_send[1, i, low] = mine.astype(BF16)
+        g_copy(5).start()
+        g_copy(1).wait_recv()
+        for i in range(2):
+            mine = wgrad_send[0, i, high].astype(F32) + wgrad_recv[2, i, high].astype(F32)
+            wgrad_send[0, i, high] = mine.astype(BF16)
+        g_copy(4).start()
 
     def pick_grads(h, c):
         out = dot(joined[0, h], w_buf[0, c], ((1,), (1,))) + dot(joined[1, h], w_buf[1, c], ((1,), (1,)))
-        router = router_ref[:, c * depth : (c + 1) * depth]
-        return out + dot(coef_hi[h], router) + dot(coef_lo[h], router)
+        part = router[:, c * depth : (c + 1) * depth]
+        return out + dot(coef_hi[h], part) + dot(coef_lo[h], part)
 
     for c in range(4):
         pick_send[:, :, c * depth : (c + 1) * depth] = pick_grads(other, c).astype(BF16).reshape(nz, half, depth)
@@ -232,7 +262,8 @@
         origin = lax.rem(z + j, nz)
         line_send[j - 1] = (pick_own[origin] + pick_recv[origin].astype(F32)).astype(BF16)
         l_copy(j).start()
-    weight_grad(s, 3)
+    weight_grad(s, wgrad_send.at[3])
+    pass_on()
 
     for j in range(1, nz):
         l_copy(j).wait_recv()
@@ -244,11 +275,11 @@
     f_copy.start()
     row_out[pl.ds(pl.multiple_of(p * half, half), half), :] = fin_send[...]
 
-    for slot in range(3):
-        g_copy(slot).wait_recv()
+    for stage in range(2, 6):
+        g_copy(stage).wait_recv()
     for i, out in enumerate((gate_out, up_out)):
         sums = wgrad_send[3, i].astype(F32)
-        for slot in range(3):
+        for slot in range(2):
             sums = sums + wgrad_recv[slot, i].astype(F32)
         out[0] = sums.astype(BF16)
     f_copy.wait_recv()
@@ -263,8 +294,8 @@
                 pl.when(goes(up, k))(z_copy(up, k, a).wait_send)
             for k in range(1, nz):
                 pl.when(comes(up, k))(q_copy(up, k, a, True).wait_send)
-    for slot in range(3):
-        g_copy(slot).wait_send()
+    for stage in range(6):
+        g_copy(stage).wait_send()
     p_copy.wait_send()
     for j in range(1, nz):
         l_copy(j).wait_send()
@@ -276,9 +307,7 @@
 ):
     rows, width = cotangent.shape
     half, depth, units = rows // 2, gate_weight.shape[1], gate_weight.shape[2]
-    spots = (positions % byte_states.shape[0])[:, None]
-    meta = jnp.pad(picks.astype(BF16), ((0, 0), (0, LANES - picks.shape[1])))
-    router = jnp.pad(router_weight.T, ((0, LANES - router_weight.shape[1]), (0, 0)))
+    spots = positions[None, :]
     vmem, dma = pltpu.VMEM, pltpu.SemaphoreType.DMA
     whole = pl.BlockSpec(memory_space=vmem)
     scratch = [
@@ -300,12 +329,13 @@
         vmem((3, 2, depth, units), BF16),
         vmem((half, width), BF16),
         vmem((half, width), BF16),
+        vmem((LANES, width), BF16),
         dma((4, 3)), dma((4, 3)),
         dma((2, nz - 1, 2)), dma((2, nz - 1, 2)),
         dma((2, nz - 1, 2)), dma((2, nz - 1, 2)),
         dma, dma,
         dma((nz - 1,)), dma((nz - 1,)),
-        dma((3,)), dma((3,)),
+        dma((6,)), dma((6,)),
         dma, dma,
     ]
     return pl.pallas_call(
@@ -321,7 +351,7 @@
         compiler_params=pltpu.CompilerParams(
             collective_id=0, has_side_effects=True, vmem_limit_bytes=52 * 2**20
         ),
-    )(byte_states, spots, meta, cotangent, router, gate_weight, up_weight, down_weight)
+    )(byte_states, spots, picks.T, cotangent, router_weight.T, gate_weight, up_weight, down_weight)
 
 
 def local(

time: 96.4 us -> 87.8 us (0.911)
  the two profiles are of different devices: /device:TPU:0 before, /device:TPU:9 now
where the time goes in v3:
time: 87.8 us; the launch traced here: 87.5 us
  Pallas kernels  79.1 us (90%)
  local copies, waits for them, and re-layouts  7.74 us (9%)
    pallas_call x1, Pallas kernels, dense(): pl.pallas_call(kernel, out_shape=(jax.ShapeDtypeStruct((rows, width), BF1...  79.1 us
    unnamed x15, local copies, waits for them, and re-layouts  7.74 us

profile of v3, /device:TPU:9, one launch (start us, length us, event | category | flops | bytes accessed | tf_op | source)
XLA Modules:
  0.0 87.5 jit_solution(5937835584315705038)
XLA Ops:
  0.6 0.0 copy-start.4
  0.6 0.0 copy-start.5
  0.7 0.7 copy-done.4
  1.3 0.0 copy-done.5
  1.3 0.0 copy-start
  1.3 1.0 %copy-done = bf16[1,512,384]{2,1,0:T(8,128)(2,1)S(1)} copy-done((bf16[1,512,384]{2,1,0:T(8,128)(2,1)S(1)}, bf16[1,512,384]{2,1,0:T(8,128)(2,1)}, u32[]{:S(2)}) %copy-start) | copy-done | bytes 393240
  2.3 0.0 copy-start.1
  2.3 1.0 %copy-done.1 = bf16[1,512,384]{2,1,0:T(8,128)(2,1)S(1)} copy-done((bf16[1,512,384]{2,1,0:T(8,128)(2,1)S(1)}, bf16[1,512,384]{2,1,0:T(8,128)(2,1)}, u32[]{:S(2)}) %copy-start.1) | copy-done | bytes 393240
  3.3 0.0 copy-start.2
  3.3 1.0 %copy-done.2 = bf16[1,512,384]{2,1,0:T(8,128)(2,1)S(1)} copy-done((bf16[1,512,384]{2,1,0:T(8,128)(2,1)S(1)}, bf16[1,512,384]{2,1,0:T(8,128)(2,1)}, u32[]{:S(2)}) %copy-start.2) | copy-done | bytes 393240
  4.3 0.0 copy-start.3
  4.3 0.7 copy-done.3
  5.0 79.1 %shard_map.103 = (bf16[128,2048]{1,0:T(8,128)(2,1)}, bf16[1,512,384]{2,1,0:T(8,128)(2,1)S(1)}, bf16[1,512,384]{2,1,0:T(8,128)(2,1)S(1)}) custom-call(bf16[256,2048]{1,0:T(8,128)(2,1)} %byte_ref.1, s32[1,128]{1,0:T(1,128)S(1)} %bitcast.5, s32[2,128]{1,0:T(2,128)S(1)} %bitcast.4, bf16[128,2048]{1,0:T(8,128)(2,1)} %cot_ref.1, bf16[4,2048]{1,0:T(4,128)(2,1)S(1)} %bitcast.3, ...), custom_call_target="tpu_custom_call" | custom-call | tf_op jit(solution)/shard_map/pallas_call | solution.py:341
  84.1 1.9 %copy.14 = bf16[128,2048]{1,0:T(8,128)(2,1)} copy(bf16[128,2048]{1,0:T(8,128)(2,1)} %get-tuple-element.6) | data formatting | bytes 1048576
  86.0 0.7 copy.15
  86.7 0.7 copy.16
Async XLA Ops:
  0.6 0.7 copy-start.4
  0.6 0.7 copy-start.5
  1.3 1.0 %copy-start = (bf16[1,512,384]{2,1,0:T(8,128)(2,1)S(1)}, bf16[1,512,384]{2,1,0:T(8,128)(2,1)}, u32[]{:S(2)}) copy-start(bf16[1,512,384]{2,1,0:T(8,128)(2,1)} %gate_ref.1) | copy-start | bytes 1179652
  2.3 1.0 %copy-start.1 = (bf16[1,512,384]{2,1,0:T(8,128)(2,1)S(1)}, bf16[1,512,384]{2,1,0:T(8,128)(2,1)}, u32[]{:S(2)}) copy-start(bf16[1,512,384]{2,1,0:T(8,128)(2,1)} %up_ref.1) | copy-start | bytes 1179652
  3.3 1.0 %copy-start.2 = (bf16[1,512,384]{2,1,0:T(8,128)(2,1)S(1)}, bf16[1,512,384]{2,1,0:T(8,128)(2,1)}, u32[]{:S(2)}) copy-start(bf16[1,512,384]{2,1,0:T(8,128)(2,1)} %down_ref.1) | copy-start | bytes 1179652
  4.3 0.7 copy-start.3

commit v4 on v3

--- a/solution.py
+++ b/solution.py
@@ -20,8 +20,8 @@
     byte_ref, pos_ref, pick_ref, cot_ref, router_ref, gate_ref, up_ref, down_ref,
     row_out, gate_out, up_out,
     x_buf, c_buf, w_buf, acc, joined, mix_buf, turn_buf, coef_hi, coef_lo,
-    pick_send, pick_recv, pick_own, line_send, line_recv, wgrad_send, wgrad_recv, fin_send, fin_recv, router,
-    w_ss, w_rs, z_ss, z_rs, q_ss, q_rs, p_ss, p_rs, l_ss, l_rs, g_ss, g_rs, f_ss, f_rs,
+    pick_send, pick_recv, pick_own, line_send, line_recv, wgrad_send, wgrad_recv, fin_send, fin_recv, router, byte_buf, hid_buf,
+    w_ss, w_rs, z_ss, z_rs, q_ss, q_rs, p_ss, p_rs, l_ss, l_rs, g_ss, g_rs, f_ss, f_rs, o_s,
 ):
     z, s, p = lax.axis_index("expert"), lax.axis_index("dp"), lax.axis_index("pair")
     nz, half, width = x_buf.shape[1], x_buf.shape[2], c_buf.shape[3]
@@ -42,22 +42,15 @@
     for peer in peers:
         pl.semaphore_signal(barrier, inc=1, device_id=peer, device_id_type=MESH)
 
-    count = byte_ref.shape[0]
-    spots = lax.broadcasted_iota(jnp.int32, (count, 2 * half), 0) + (z * 4 + s) * count
-    hot = jnp.where(spots == pos_ref[...], 1.0, 0.0).astype(BF16)
-    for c in range(0, width, depth):
-        rows = dot(hot, byte_ref[:, c : c + depth], ((0,), (0,))).astype(BF16)
-        for h in range(2):
-            x_buf[h, z, :, c : c + depth] = rows[h * half : (h + 1) * half]
-    place = lax.broadcasted_iota(jnp.int32, (LANES, 2 * half), 0)
-    picked = pick_ref[...].astype(F32)
-    meta = jnp.where(place == 0, picked[0:1, :], jnp.where(place == 1, picked[1:2, :], 0.0)).T
-    for h in range(2):
-        x_buf[h, z, :, width:] = meta[h * half : (h + 1) * half].astype(BF16)
-        c_buf[h, z] = cot_ref[h * half : (h + 1) * half, :]
+    own = [gate_ref.at[0], up_ref.at[0], down_ref.at[0]]
+    local_copies = [
+        pltpu.make_async_copy(cot_ref.at[pl.ds(h * half, half)], c_buf.at[h, z], o_s.at[h]) for h in range(2)
+    ]
+    local_copies += [pltpu.make_async_copy(byte_ref, byte_buf, o_s.at[2])]
+    local_copies += [pltpu.make_async_copy(own[i], w_buf.at[i, s], o_s.at[3 + i]) for i in range(3)]
+    for one in local_copies:
+        one.start()
     pl.semaphore_wait(barrier, len(peers))
-
-    own = [gate_ref.at[0], up_ref.at[0], down_ref.at[0]]
 
     def w_copy(kind, i):
         if kind == 0:
@@ -109,9 +102,26 @@
         there = z + 1 < nz if up else z >= 1
         return jnp.logical_and(there, comes(up, k)) if k else there
 
-    for a in range(2):
-        for up in (True, False):
-            pl.when(goes(up, 0))(z_copy(up, 0, a).start)
+    for one in local_copies[:2]:
+        one.wait()
+    for up in (True, False):
+        pl.when(goes(up, 0))(z_copy(up, 0, 0).start)
+
+    local_copies[2].wait()
+    count = byte_buf.shape[0]
+    spots = lax.broadcasted_iota(jnp.int32, (count, 2 * half), 0) + (z * 4 + s) * count
+    hot = jnp.where(spots == pos_ref[...], 1.0, 0.0).astype(BF16)
+    for c in range(0, width, depth):
+        rows = dot(hot, byte_buf[:, c : c + depth], ((0,), (0,))).astype(BF16)
+        for h in range(2):
+            x_buf[h, z, :, c : c + depth] = rows[h * half : (h + 1) * half]
+    place = lax.broadcasted_iota(jnp.int32, (LANES, 2 * half), 0)
+    picked = pick_ref[...].astype(F32)
+    meta = jnp.where(place == 0, picked[0:1, :], jnp.where(place == 1, picked[1:2, :], 0.0)).T
+    for h in range(2):
+        x_buf[h, z, :, width:] = meta[h * half : (h + 1) * half].astype(BF16)
+    for up in (True, False):
+        pl.when(goes(up, 0))(z_copy(up, 0, 1).start)
 
     def z_step(k):
         for a in range(2):
@@ -131,8 +141,8 @@
         w_arrived(1, i)
         w_copy(3, i).start()
 
-    for i in range(3):
-        w_buf[i, s] = own[i][...]
+    for one in local_copies[3:]:
+        one.wait()
     router[...] = jnp.zeros_like(router)
     router[: router_ref.shape[0], :] = router_ref[...]
     z_step(1)
@@ -173,7 +183,7 @@
     accumulate(s, True)
     accumulate(x_nb, False)
     accumulate(y_nb, False)
-    for i in range(3):
+    for i in range(2):
         w_arrived(2, i)
         w_arrived(3, i)
         accumulate(diag, False, (i,))
@@ -184,19 +194,25 @@
     def _(n):
         part = pl.ds(pl.multiple_of(n * step, step), step)
         for h in range(2):
-            gate, up, cot_down = acc[0, h, part], acc[1, h, part], acc[2, h, part]
+            gate, up = acc[0, h, part], acc[1, h, part]
             sigma = jax.nn.sigmoid(gate)
             activ = gate * sigma
             slope = sigma * (1.0 + gate * (1.0 - sigma))
-            hidden = (activ * up).astype(BF16).astype(F32)
-            mix_part = jnp.sum(hidden * cot_down, axis=1, keepdims=True)
-            grad = mix_buf[h, part] * cot_down
-            joined[0, h, part] = (grad * up * slope).astype(BF16)
-            joined[1, h, part] = (grad * activ).astype(BF16)
-            coef = mix_part * turn_buf[h, part]
-            high = coef.astype(BF16)
-            coef_hi[h, part] = high
-            coef_lo[h, part] = (coef - high.astype(F32)).astype(BF16)
+            hid_buf[h, part] = (activ * up).astype(BF16)
+            acc[0, h, part] = mix_buf[h, part] * (up * slope)
+            acc[1, h, part] = mix_buf[h, part] * activ
+
+    w_arrived(2, 2)
+    w_arrived(3, 2)
+    accumulate(diag, False, (2,))
+
+    @pl.loop(0, nz * half // step)
+    def _(n):
+        part = pl.ds(pl.multiple_of(n * step, step), step)
+        for h in range(2):
+            cot_down = acc[2, h, part]
+            joined[0, h, part] = (cot_down * acc[0, h, part]).astype(BF16)
+            joined[1, h, part] = (cot_down * acc[1, h, part]).astype(BF16)
 
     low, high = pl.ds(0, depth // 2), pl.ds(depth // 2, depth // 2)
 
@@ -240,6 +256,16 @@
             mine = wgrad_send[0, i, high].astype(F32) + wgrad_recv[2, i, high].astype(F32)
             wgrad_send[0, i, high] = mine.astype(BF16)
         g_copy(4).start()
+
+    @pl.loop(0, nz * half // step)
+    def _(n):
+        part = pl.ds(pl.multiple_of(n * step, step), step)
+        for h in range(2):
+            mix_part = jnp.sum(hid_buf[h, part].astype(F32) * acc[2, h, part], axis=1, keepdims=True)
+            coef = mix_part * turn_buf[h, part]
+            top = coef.astype(BF16)
+            coef_hi[h, part] = top
+            coef_lo[h, part] = (coef - top.astype(F32)).astype(BF16)
 
     def pick_grads(h, c):
         out = dot(joined[0, h], w_buf[0, c], ((1,), (1,))) + dot(joined[1, h], w_buf[1, c], ((1,), (1,)))
@@ -309,7 +335,7 @@
     half, depth, units = rows // 2, gate_weight.shape[1], gate_weight.shape[2]
     spots = positions[None, :]
     vmem, dma = pltpu.VMEM, pltpu.SemaphoreType.DMA
-    whole = pl.BlockSpec(memory_space=vmem)
+    whole, far = pl.BlockSpec(memory_space=vmem), pl.BlockSpec(memory_space=pl.ANY)
     scratch = [
         vmem((2, nz, half, width + LANES), BF16),
         vmem((2, nz, half, width), BF16),
@@ -330,6 +356,8 @@
         vmem((half, width), BF16),
         vmem((half, width), BF16),
         vmem((LANES, width), BF16),
+        vmem(byte_states.shape, BF16),
+        vmem((2, nz * half, units), BF16),
         dma((4, 3)), dma((4, 3)),
         dma((2, nz - 1, 2)), dma((2, nz - 1, 2)),
         dma((2, nz - 1, 2)), dma((2, nz - 1, 2)),
@@ -337,6 +365,7 @@
         dma((nz - 1,)), dma((nz - 1,)),
         dma((6,)), dma((6,)),
         dma, dma,
+        dma((6,)),
     ]
     return pl.pallas_call(
         kernel,
@@ -345,11 +374,11 @@
             jax.ShapeDtypeStruct(gate_weight.shape, BF16),
             jax.ShapeDtypeStruct(up_weight.shape, BF16),
         ),
-        in_specs=[whole] * 8,
+        in_specs=[far, whole, whole, far, whole, far, far, far],
         out_specs=(whole,) * 3,
         scratch_shapes=scratch,
         compiler_params=pltpu.CompilerParams(
-            collective_id=0, has_side_effects=True, vmem_limit_bytes=52 * 2**20
+            collective_id=0, has_side_effects=True, vmem_limit_bytes=58 * 2**20
         ),
     )(byte_states, spots, picks.T, cotangent, router_weight.T, gate_weight, up_weight, down_weight)
 

time: 87.8 us -> 83.5 us (0.951)
  local copies, waits for them, and re-layouts: 7.74 us -> 3.82 us
    unnamed x15 -> x7, local copies, waits for them, and re-layouts: 7.74 us -> 3.82 us
where the time goes in v4:
time: 83.5 us; the launch traced here: 83.3 us
  Pallas kernels  78.8 us (94%)
  local copies, waits for them, and re-layouts  3.82 us (5%)
    pallas_call x1, Pallas kernels, dense(): pl.pallas_call(kernel, out_shape=(jax.ShapeDtypeStruct((rows, width), BF1...  78.8 us
    unnamed x7, local copies, waits for them, and re-layouts  3.82 us

profile of v4, /device:TPU:9, one launch (start us, length us, event | category | flops | bytes accessed | tf_op | source)
XLA Modules:
  0.0 83.3 jit_solution(13059597232482364754)
XLA Ops:
  0.6 78.8 %shard_map.103 = (bf16[128,2048]{1,0:T(8,128)(2,1)}, bf16[1,512,384]{2,1,0:T(8,128)(2,1)}, bf16[1,512,384]{2,1,0:T(8,128)(2,1)}) custom-call(bf16[256,2048]{1,0:T(8,128)(2,1)} %byte_ref.1, s32[1,128]{1,0:T(1,128)} %bitcast.5, s32[2,128]{1,0:T(2,128)} %bitcast.4, bf16[128,2048]{1,0:T(8,128)(2,1)} %cot_ref.1, bf16[4,2048]{1,0:T(4,128)(2,1)} %bitcast.3, ...), custom_call_target="tpu_custom_call" | custom-call | tf_op jit(solution)/shard_map/pallas_call | solution.py:370
  79.4 0.0 copy-start.1
  79.4 1.9 %copy.14 = bf16[128,2048]{1,0:T(8,128)(2,1)} copy(bf16[128,2048]{1,0:T(8,128)(2,1)} %get-tuple-element.6) | data formatting | bytes 1048576
  81.4 0.0 copy-done.1
  81.4 0.0 copy-start
  81.4 0.7 copy.15
  82.1 0.4 copy-done
  82.5 0.7 copy.16
Async XLA Ops:
  79.4 1.9 %copy-start.1 = (bf16[1,512,384]{2,1,0:T(8,128)(2,1)S(1)}, bf16[1,512,384]{2,1,0:T(8,128)(2,1)}, u32[]{:S(2)}) copy-start(bf16[1,512,384]{2,1,0:T(8,128)(2,1)} %get-tuple-element.7) | copy-start | bytes 1179652
  81.4 1.1 %copy-start = (bf16[1,512,384]{2,1,0:T(8,128)(2,1)S(1)}, bf16[1,512,384]{2,1,0:T(8,128)(2,1)}, u32[]{:S(2)}) copy-start(bf16[1,512,384]{2,1,0:T(8,128)(2,1)} %get-tuple-element.8) | copy-start | bytes 1179652

commit v5 on v4

--- a/solution.py
+++ b/solution.py
@@ -216,7 +216,7 @@
 
     low, high = pl.ds(0, depth // 2), pl.ds(depth // 2, depth // 2)
 
-    def weight_grad(owner, keep):
+    def weight_grad(owner, keep, stages=()):
         cols = pl.ds(pl.multiple_of(owner * depth, depth), depth)
         for i in range(2):
             total = None
@@ -225,37 +225,31 @@
                 term = dot(x, joined[i, h], ((0,), (0,)))
                 total = term if total is None else total + term
             keep[i] = total.astype(BF16)
-
-    def g_copy(stage):
+            for stage in stages:
+                g_copy(stage, i).start()
+
+    def g_copy(stage, i):
         to_x = stage % 2 == 0
         slot = 2 if stage < 2 else 0 if to_x else 1
         part = low if stage in (0, 2, 5) else high
-        src = wgrad_send.at[slot, :, part]
+        src = wgrad_send.at[slot, i, part]
         if stage < 2:
-            dst = wgrad_recv.at[2, :, part]
+            dst = wgrad_recv.at[2, i, part]
         else:
-            dst = wgrad_recv.at[0 if to_x else 1, :, part]
-        return copy(src, dst, g_ss.at[stage], g_rs.at[stage], {"dp": x_nb if to_x else y_nb})
-
-    weight_grad(diag, wgrad_send.at[2])
-    g_copy(0).start()
-    g_copy(1).start()
-    weight_grad(x_nb, wgrad_send.at[0])
-    g_copy(2).start()
-    weight_grad(y_nb, wgrad_send.at[1])
-    g_copy(3).start()
+            dst = wgrad_recv.at[0 if to_x else 1, i, part]
+        return copy(src, dst, g_ss.at[stage, i], g_rs.at[stage, i], {"dp": x_nb if to_x else y_nb})
+
+    weight_grad(diag, wgrad_send.at[2], (0, 1))
+    weight_grad(x_nb, wgrad_send.at[0], (2,))
+    weight_grad(y_nb, wgrad_send.at[1], (3,))
 
     def pass_on():
-        g_copy(0).wait_recv()
         for i in range(2):
-            mine = wgrad_send[1, i, low].astype(F32) + wgrad_recv[2, i, low].astype(F32)
-            wgrad_send[1, i, low] = mine.astype(BF16)
-        g_copy(5).start()
-        g_copy(1).wait_recv()
-        for i in range(2):
-            mine = wgrad_send[0, i, high].astype(F32) + wgrad_recv[2, i, high].astype(F32)
-            wgrad_send[0, i, high] = mine.astype(BF16)
-        g_copy(4).start()
+            for came, slot, part, stage in ((0, 1, low, 5), (1, 0, high, 4)):
+                g_copy(came, i).wait_recv()
+                mine = wgrad_send[slot, i, part].astype(F32) + wgrad_recv[2, i, part].astype(F32)
+                wgrad_send[slot, i, part] = mine.astype(BF16)
+                g_copy(stage, i).start()
 
     @pl.loop(0, nz * half // step)
     def _(n):
@@ -302,7 +296,8 @@
     row_out[pl.ds(pl.multiple_of(p * half, half), half), :] = fin_send[...]
 
     for stage in range(2, 6):
-        g_copy(stage).wait_recv()
+        for i in range(2):
+            g_copy(stage, i).wait_recv()
     for i, out in enumerate((gate_out, up_out)):
         sums = wgrad_send[3, i].astype(F32)
         for slot in range(2):
@@ -321,7 +316,8 @@
             for k in range(1, nz):
                 pl.when(comes(up, k))(q_copy(up, k, a, True).wait_send)
     for stage in range(6):
-        g_copy(stage).wait_send()
+        for i in range(2):
+            g_copy(stage, i).wait_send()
     p_copy.wait_send()
     for j in range(1, nz):
         l_copy(j).wait_send()
@@ -363,7 +359,7 @@
         dma((2, nz - 1, 2)), dma((2, nz - 1, 2)),
         dma, dma,
         dma((nz - 1,)), dma((nz - 1,)),
-        dma((6,)), dma((6,)),
+        dma((6, 2)), dma((6, 2)),
         dma, dma,
         dma((6,)),
     ]

time: 83.5 us -> 84.2 us (level)
  no operation moved by 1% of the time
where the time goes in v5:
time: 84.2 us; the launch traced here: 84 us
  Pallas kernels  79.5 us (94%)
  local copies, waits for them, and re-layouts  3.82 us (5%)
    pallas_call x1, Pallas kernels, dense(): pl.pallas_call(kernel, out_shape=(jax.ShapeDtypeStruct((rows, width), BF1...  79.5 us
    unnamed x7, local copies, waits for them, and re-layouts  3.82 us

profile of v5, /device:TPU:9, one launch (start us, length us, event | category | flops | bytes accessed | tf_op | source)
XLA Modules:
  0.0 84.0 jit_solution(16531170923540982006)
XLA Ops:
  0.6 79.5 %shard_map.103 = (bf16[128,2048]{1,0:T(8,128)(2,1)}, bf16[1,512,384]{2,1,0:T(8,128)(2,1)}, bf16[1,512,384]{2,1,0:T(8,128)(2,1)}) custom-call(bf16[256,2048]{1,0:T(8,128)(2,1)} %byte_ref.1, s32[1,128]{1,0:T(1,128)} %bitcast.5, s32[2,128]{1,0:T(2,128)} %bitcast.4, bf16[128,2048]{1,0:T(8,128)(2,1)} %cot_ref.1, bf16[4,2048]{1,0:T(4,128)(2,1)} %bitcast.3, ...), custom_call_target="tpu_custom_call" | custom-call | tf_op jit(solution)/shard_map/pallas_call | solution.py:366
  80.1 0.0 copy-start.1
  80.1 1.9 %copy.14 = bf16[128,2048]{1,0:T(8,128)(2,1)} copy(bf16[128,2048]{1,0:T(8,128)(2,1)} %get-tuple-element.6) | data formatting | bytes 1048576
  82.1 0.0 copy-done.1
  82.1 0.0 copy-start
  82.1 0.7 copy.15
  82.8 0.4 copy-done
  83.2 0.7 copy.16
Async XLA Ops:
  80.1 1.9 %copy-start.1 = (bf16[1,512,384]{2,1,0:T(8,128)(2,1)S(1)}, bf16[1,512,384]{2,1,0:T(8,128)(2,1)}, u32[]{:S(2)}) copy-start(bf16[1,512,384]{2,1,0:T(8,128)(2,1)} %get-tuple-element.7) | copy-start | bytes 1179652
  82.1 1.1 %copy-start = (bf16[1,512,384]{2,1,0:T(8,128)(2,1)S(1)}, bf16[1,512,384]{2,1,0:T(8,128)(2,1)}, u32[]{:S(2)}) copy-start(bf16[1,512,384]{2,1,0:T(8,128)(2,1)} %get-tuple-element.8) | copy-start | bytes 1179652
